TPU v7x, 512 devices: a whole 4x4x16 slice. The times are simulated.
512 devices in a mesh: row: 8 (over y, core), col: 16 (over z_hi, x), rep: 4 (over z_lo).
Axes of the slice: x: 4, y: 4, z: 16 (z_hi: 4, z_lo: 4; z = z_hi * 4 + z_lo), core: 2. Of those that a mesh axis runs over, the one named last changes fastest.
Arguments:
- amplitudes: bfloat16 [6144, 100, 1024], P(('row', 'col'), 'rep'), may hold values from -6 to 6
- integrals: bfloat16 [100, 1024, 1024], P('rep', 'col', 'row'), may hold values from -0.02734375 to 0.02734375
Outputs:
- cycle: float32 [6144, 1024], P('row', ('col', 'rep'))
All inputs are finite; a program needn't handle non-finite values.
Results may differ from a plain program's by a relative error of at most 0.0003.
Values may be sent and summed in bfloat16 or wider, within the bound.
No kernel may reach another device: no remote copies, remote signals or barrier semaphores. Data moves between devices by JAX's collectives and lax.ppermute only.
A program may use at most 64 MiB of HBM per device.

v0:
```python
import jax
import jax.numpy as jnp
from jax import lax
from jax.sharding import PartitionSpec as P


def local(amplitudes, integrals):
    remapped = lax.all_to_all(amplitudes, "col", split_axis=2, concat_axis=0, tiled=True)
    row_count = remapped.shape[0]
    flattened = remapped.reshape(row_count, -1)
    columns = lax.all_gather(integrals, "row", axis=2, tiled=True).reshape(flattened.shape[1], -1)
    partial_value = jnp.dot(flattened, columns, preferred_element_type=jnp.float32)
    summed = lax.psum_scatter(partial_value, ("col", "rep"), scatter_dimension=1, tiled=True)
    return summed


def solution(mesh):
    return jax.shard_map(
        local,
        mesh=mesh,
        in_specs=(P(("row", "col"), "rep", None), P("rep", "col", "row")),
        out_specs=P("row", ("col", "rep")),
        check_vma=False,
    )
```

profile of v0, /device:TPU:24, one launch (start us, length us, event | category | flops | bytes accessed | tf_op | source)
XLA Modules:
  0.0 503.2 jit_solution(9052632418614310384)
XLA Ops:
  6.5 12.9 %copy.4 = bf16[48,25,1024]{0,1,2:T(8,128)(2,1)} copy(bf16[48,25,1024]{2,0,1:T(8,128)(2,1)} %param.2) | data formatting | bytes 4915200 | tf_op args[0]
  19.4 14.9 %reshape.9 = bf16[16,2,38400]{2,1,0:T(2,128)(2,1)} reshape(bf16[1024,25,48]{2,1,0:T(8,128)(2,1)} %bitcast.8) | data formatting | bytes 4915200
  34.2 17.7 %all-to-all-start = ((bf16[16,2,38400]{2,1,0:T(2,128)(2,1)}), bf16[16,2,38400]{2,1,0:T(2,128)(2,1)S(1)}, u32[]{:S(2)}, u32[]{:S(2)}) async-start(bf16[16,2,38400]{2,1,0:T(2,128)(2,1)} %reshape.9), calls=%async_computation | async-start | bytes 4915200 | tf_op jit(solution)/shard_map/all_to_all | solution.py:8
  51.9 0.0 all-gather.2.cloned.1.call-start
  52.0 0.7 all-gather.2.cloned.1.call-update
  52.6 0.0 reduce-scatter.2.cloned.1.call-start
  52.7 110.2 %all-to-all-done = bf16[16,2,38400]{2,1,0:T(2,128)(2,1)S(1)} async-done(((bf16[16,2,38400]{2,1,0:T(2,128)(2,1)}), bf16[16,2,38400]{2,1,0:T(2,128)(2,1)S(1)}, u32[]{:S(2)}, u32[]{:S(2)}) %all-to-all-start) | async-done | bytes 2457632 | tf_op jit(solution)/shard_map/all_to_all | solution.py:8
  162.9 9.8 %reshape.10 = bf16[1024,25,48]{2,1,0:T(8,128)(2,1)} reshape(bf16[16,2,38400]{2,1,0:T(2,128)(2,1)S(1)} %all-to-all-done) | data formatting | bytes 4915200
  172.7 15.1 %copy.5 = bf16[48,25,16,64]{3,1,0,2:T(8,128)(2,1)} copy(bf16[48,25,16,64]{0,1,3,2:T(8,128)(2,1)} %bitcast.7) | data formatting | bytes 4915200 | tf_op jit(solution)/shard_map/all_to_all | solution.py:8
  187.8 7.5 %reshape.7 = bf16[768,1600]{1,0:T(8,128)(2,1)S(1)} reshape(bf16[16,48,25,64]{3,2,1,0:T(8,128)(2,1)} %bitcast.9) | data formatting | bytes 4915200 | tf_op jit(solution)/shard_map/reshape | solution.py:10
  195.4 0.0 all-gather.2.cloned.1.call-done
  195.4 6.7 %fusion = f32[768,1024]{0,1:T(8,128)} fusion(bf16[768,1600]{1,0:T(8,128)(2,1)S(1)} %reshape.7, bf16[1600,1024]{1,0:T(8,128)(2,1)} %bitcast.10), kind=kOutput, calls=%fused_computation | convolution fusion | flops 2516582400 | bytes 8880128 | tf_op jit(solution)/shard_map/dot_general | solution.py:12
  202.0 0.0 reduce-scatter.2.cloned.1.call-update
  202.1 294.3 %reduce-scatter.2.cloned.1.call-done = f32[768,16]{0,1:T(8,128)} async-done(((f32[768,1024]{0,1:T(8,128)}), f32[768,16]{0,1:T(8,128)}) %reduce-scatter.2.cloned.1.call-update) | async-done | bytes 49168 | tf_op jit(solution)/shard_map/reduce_scatter | solution.py:13
Async XLA Ops:
  34.2 128.6 %all-to-all-start = ((bf16[16,2,38400]{2,1,0:T(2,128)(2,1)}), bf16[16,2,38400]{2,1,0:T(2,128)(2,1)S(1)}, u32[]{:S(2)}, u32[]{:S(2)}) async-start(bf16[16,2,38400]{2,1,0:T(2,128)(2,1)} %reshape.9), calls=%async_computation | async-start | bytes 4915200 | tf_op jit(solution)/shard_map/all_to_all | solution.py:8
  51.9 143.5 %all-gather.2.cloned.1.call-start = ((), (), s32[]{:S(2)}) async-start(), calls=%async_computation.2 | async-start | bytes 3686400 | tf_op jit(solution)/shard_map/all_gather | solution.py:11
  52.6 443.7 %reduce-scatter.2.cloned.1.call-start = ((), (), s32[]{:S(2)}) async-start(), calls=%async_computation.3 | async-start | bytes 3194880 | tf_op jit(solution)/shard_map/reduce_scatter | solution.py:13
Sparse Core Ops, SparseCore 0:
  54.9 40.1 all-gather.1
  202.2 294.1 reduce-scatter.1
where the time goes:
time: 504 us; the launch traced here: 503 us
  waiting for transfers between devices  405 us (80%)
  local copies, waits for them, and re-layouts  60.2 us (12%)
  starting transfers between devices  17.7 us (4%)
  between operations  13.4 us (3%)
  matrix products  6.66 us (1%)
    reduce_scatter x1, waiting for transfers between devices, local(): lax.psum_scatter(partial_value, ('col', 'rep'), scatter_dimension=1, tile...  294 us
    all_to_all x1, waiting for transfers between devices, local(): lax.all_to_all(amplitudes, 'col', split_axis=2, concat_axis=0, tiled=True)  110 us
    unnamed x3, local copies, waits for them, and re-layouts  37.5 us
    all_to_all x1, starting transfers between devices, local(): lax.all_to_all(amplitudes, 'col', split_axis=2, concat_axis=0, tiled=True)  17.7 us
    all_to_all x1, local copies, waits for them, and re-layouts, local(): lax.all_to_all(amplitudes, 'col', split_axis=2, concat_axis=0, tiled=True)  15.1 us
  transfers between devices with their start and end apart: 3, of which 2 were waited for; matrix products, arithmetic and copies ran while one was open for 6% of the time, Pallas kernels for 0%

commit v1 on v0

v1 whole, which is shorter than its diff:
```python
import jax
import jax.numpy as jnp
from jax import lax
from jax.experimental import pallas as pl
from jax.experimental.pallas import tpu as pltpu
from jax.sharding import Mesh, PartitionSpec as P

BF16 = jnp.bfloat16
F32 = jnp.float32
K = 25
PAIRS = 13
DEPTH = PAIRS * 128
ROWS = 48
VMEM = pl.BlockSpec(memory_space=pltpu.VMEM)
SMEM = pl.BlockSpec(memory_space=pltpu.SMEM)


def params():
    return pltpu.CompilerParams(vmem_limit_bytes=32 * 2**20)


def reorder_kernel(a_ref, src_ref, out_ref, perm_ref):
    perm_ref[...] = (lax.broadcasted_iota(jnp.int32, (1024, 1024), 0) == src_ref[...]).astype(BF16)
    for p in range(2):
        columns = []
        for parity in range(2):
            for zh in range(4):
                at = pl.ds(zh * 256 + p * 128, 128)
                planes = [
                    a_ref[k, :, at] if k < K else jnp.zeros((ROWS, 128), BF16)
                    for k in range(parity, 2 * PAIRS, 2)
                ]
                columns.append(jnp.concatenate(planes, axis=0))
        left = jnp.concatenate(columns, axis=1)
        for y in range(4):
            moved = jnp.dot(left, perm_ref[:, y * 256:(y + 1) * 256], preferred_element_type=F32).astype(BF16)
            for xb in range(2):
                out_ref[y * 4 + 2 * p + xb] = moved[:, xb * 128:(xb + 1) * 128]


def reorder(planes, src):
    return pl.pallas_call(
        reorder_kernel,
        out_shape=jax.ShapeDtypeStruct((16, PAIRS * ROWS, 128), BF16),
        in_specs=[VMEM, VMEM],
        out_specs=VMEM,
        scratch_shapes=[pltpu.VMEM((1024, 1024), BF16)],
        compiler_params=params(),
        cost_estimate=pl.CostEstimate(flops=2 * 624 * 2048 * 1024, bytes_accessed=5 * 2**20, transcendentals=0),
        name="reorder",
    )(planes, src)


def product_kernel(core_ref, a_ref, own_ref, other_ref, out_ref, right_ref):
    core = core_ref[0]
    mine = pl.ds(pl.multiple_of(core * 128, 128), 128)
    theirs = pl.ds(pl.multiple_of((1 - core) * 128, 128), 128)
    for k in range(K):
        for zh in range(4):
            rows = pl.ds(k * 64 + zh * 16, 16)
            right_ref[rows, mine] = own_ref[zh, k]
            right_ref[rows, theirs] = other_ref[zh, k]
    right_ref[pl.ds(K * 64, 64), :] = jnp.zeros((64, 256), BF16)
    for y in range(4):
        left = jnp.concatenate(
            [a_ref[4 * y:4 * y + 4, p * ROWS:(p + 1) * ROWS, :].reshape(192, 128) for p in range(PAIRS)], axis=1
        )
        block = jnp.dot(left, right_ref[...], preferred_element_type=F32)
        for x in range(4):
            part = block[:, x * 64:(x + 1) * 64]
            out_ref[y * 4 + x] = jnp.concatenate([part[:96], part[96:]], axis=1)


def product(core, a, own, other):
    return pl.pallas_call(
        product_kernel,
        out_shape=jax.ShapeDtypeStruct((16, 96, 128), F32),
        in_specs=[SMEM, VMEM, VMEM, VMEM],
        out_specs=VMEM,
        scratch_shapes=[pltpu.VMEM((DEPTH, 256), BF16)],
        compiler_params=params(),
        cost_estimate=pl.CostEstimate(flops=2 * 768 * DEPTH * 256, bytes_accessed=5 * 2**20, transcendentals=0),
        name="product",
    )(core, a, own, other)


def first_sum_kernel(*refs):
    out_ref = refs[-1]
    for zh in range(4):
        total = jnp.sum(refs[zh][...], axis=0)
        turned = total.T
        for zl in range(4):
            at = zl * 16
            out_ref[zh * 4 + zl, :16, :96] = turned[at:at + 16]
            out_ref[zh * 4 + zl, 16:, :96] = turned[64 + at:64 + at + 16]
            out_ref[zh * 4 + zl, :, 96:] = jnp.zeros((32, 32), F32)


def first_sum(parts):
    return pl.pallas_call(
        first_sum_kernel,
        out_shape=jax.ShapeDtypeStruct((16, 32, 128), F32),
        in_specs=[VMEM] * 4,
        out_specs=VMEM,
        compiler_params=params(),
        cost_estimate=pl.CostEstimate(flops=2**20, bytes_accessed=4 * 2**20, transcendentals=0),
        name="first_sum",
    )(*parts)


def last_sum_kernel(in_ref, out_ref):
    for zh in range(4):
        total = in_ref[4 * zh] + in_ref[4 * zh + 1] + in_ref[4 * zh + 2] + in_ref[4 * zh + 3]
        for half in range(2):
            out_ref[:, zh * 192 + half * 96:zh * 192 + half * 96 + 96] = total[half * 16:half * 16 + 16, :96]


def last_sum(parts):
    return pl.pallas_call(
        last_sum_kernel,
        out_shape=jax.ShapeDtypeStruct((16, 768), F32),
        in_specs=[VMEM],
        out_specs=VMEM,
        compiler_params=params(),
        cost_estimate=pl.CostEstimate(flops=2**16, bytes_accessed=2**19, transcendentals=0),
        name="last_sum",
    )(parts)


def source_of_lane():
    lane = jnp.arange(1024, dtype=jnp.int32)
    y, xb, parity, zh, i = lane // 256, lane // 128 % 2, lane // 64 % 2, lane // 16 % 4, lane % 16
    return (parity * 512 + zh * 128 + xb * 64 + y * 16 + i).reshape(1, 1024)


def local(amplitudes, integrals):
    core = lax.axis_index("core").astype(jnp.int32).reshape(1)
    by_y = integrals.reshape(K, 4, 16, 128).transpose(1, 0, 2, 3)
    blocks = lax.all_to_all(by_y, "y", 0, 0, tiled=True)
    gathered = lax.all_gather(blocks, "zh", axis=0, tiled=False)

    sent = reorder(amplitudes.transpose(1, 0, 2), source_of_lane())
    rows = lax.all_to_all(sent, ("y", "x"), 0, 0, tiled=True)

    swapped = lax.ppermute(gathered, "core", [(0, 1), (1, 0)])
    partial = [product(core, rows, gathered[:, c], swapped[:, c]) for c in range(4)]
    arrived = [lax.all_to_all(part, ("y", "x"), 0, 0, tiled=True) for part in partial]
    final = lax.all_to_all(first_sum(arrived), ("zh", "zl"), 0, 0, tiled=True)
    return last_sum(final).T


def solution(mesh):
    fine = Mesh(mesh.devices.reshape(4, 2, 4, 4, 4), ("y", "core", "zh", "x", "zl"))
    return jax.shard_map(
        local,
        mesh=fine,
        in_specs=(P(("y", "core", "zh", "x"), "zl", None), P("zl", ("zh", "x"), ("y", "core"))),
        out_specs=P(("y", "core"), ("zh", "x", "zl")),
        check_vma=False,
    )
```

time: 504 us -> 218 us (0.43)
  waiting for transfers between devices: 405 us -> 91.9 us
  blocking collectives: 0 us -> 51.5 us
  local copies, waits for them, and re-layouts: 60.2 us -> 18.2 us
  Pallas kernels: 0 us -> 12.5 us
  starting transfers between devices: 17.7 us -> 27.8 us
  matrix products: 6.66 us -> 0 us
    reduce_scatter x1 -> x0, waiting for transfers between devices: 294 us -> none  [local(): lax.psum_scatter(partial_value, ('col', 'rep'), scatter_dimension=1, tile...]
    all_to_all x1 -> x4, waiting for transfers between devices: 110 us -> 22.9 us  [the longest x3 22.9 us: local(): lax.all_to_all(part, ('y', 'x'), 0, 0, tiled=True)]
    all_gather x1, waiting for transfers between devices: 0.02 us -> 67.8 us  [local(): gathered = lax.all_gather(blocks, 'zh', axis=0, tiled=False)]
    all_to_all x0 -> x3, blocking collectives: none -> 51.5 us  [the longest x1 22.5 us: local(): final = lax.all_to_all(first_sum(arrived), ('zh', 'zl'), 0, 0, tiled=True)]
    unnamed x3 -> x20, local copies, waits for them, and re-layouts: 37.5 us -> 9.16 us
    all_to_all x1 -> x0, local copies, waits for them, and re-layouts: 15.1 us -> none  [local(): lax.all_to_all(amplitudes, 'col', split_axis=2, concat_axis=0, tiled=True)]
    pallas_call x0 -> x7, Pallas kernels: none -> 12.5 us  [the longest x4 7.25 us: product(): pl.pallas_call(product_kernel, out_shape=jax.ShapeDtypeStruct((16, 96, 12...]
    all_to_all x1 -> x4, starting transfers between devices: 17.7 us -> 25.9 us  [the longest x3 20.2 us: local(): lax.all_to_all(part, ('y', 'x'), 0, 0, tiled=True)]
  transfers between devices with their start and end apart: 3 -> 6, of which waited for: 2 -> 5; matrix products, arithmetic and copies ran while one was open for 6% -> 4% of each run, Pallas kernels for 0% -> 4%
where the time goes in v1:
time: 218 us; the launch traced here: 215 us
  waiting for transfers between devices  91.9 us (42%)
  blocking collectives  51.5 us (24%)
  starting transfers between devices  27.8 us (13%)
  local copies, waits for them, and re-layouts  18.2 us (8%)
  between operations  13.5 us (6%)
  Pallas kernels  12.5 us (6%)
    all_gather x1, waiting for transfers between devices, local(): gathered = lax.all_gather(blocks, 'zh', axis=0, tiled=False)  67.8 us
    all_to_all x3, waiting for transfers between devices, local(): lax.all_to_all(part, ('y', 'x'), 0, 0, tiled=True)  22.9 us
    all_to_all x1, blocking collectives, local(): final = lax.all_to_all(first_sum(arrived), ('zh', 'zl'), 0, 0, tiled=True)  22.5 us
    all_to_all x3, starting transfers between devices, local(): lax.all_to_all(part, ('y', 'x'), 0, 0, tiled=True)  20.2 us
    all_to_all x1, blocking collectives, local(): lax.all_to_all(part, ('y', 'x'), 0, 0, tiled=True)  15 us
    all_to_all x1, blocking collectives, local(): blocks = lax.all_to_all(by_y, 'y', 0, 0, tiled=True)  14.1 us
    unnamed x20, local copies, waits for them, and re-layouts  9.16 us
    pallas_call x4, Pallas kernels, product(): pl.pallas_call(product_kernel, out_shape=jax.ShapeDtypeStruct((16, 96, 12...  7.25 us
  transfers between devices with their start and end apart: 6, of which 5 were waited for; matrix products, arithmetic and copies ran while one was open for 4% of the time, Pallas kernels for 4%

profile of v1, /device:TPU:24, one launch (start us, length us, event | category | flops | bytes accessed | tf_op | source)
XLA Modules:
  0.0 215.5 jit_solution(6554865579388310971)
XLA Ops:
  6.5 0.0 all-gather.3.cloned.1.call-start
  6.5 1.0 copy.20
  7.6 14.1 %all_to_all.35 = bf16[4,25,16,128]{3,2,1,0:T(8,128)(2,1)} all-to-all(bf16[4,25,16,128]{3,2,1,0:T(8,128)(2,1)S(1)} %copy.20), channel_id=1, replica_groups=mesh['y'=4,'core'=2,'zh'=4,'x'=4,'zl'=4] {'y'}, dimensions={0} | all-to-all | bytes 819200 | tf_op jit(solution)/shard_map/all_to_all | solution.py:139
  21.6 0.0 all-gather.3.cloned.1.call-update
  21.7 0.0 copy-start.9
  21.7 1.7 copy-done.9
  23.4 3.0 %reorder.1 = bf16[16,624,128]{2,1,0:T(8,128)(2,1)S(1)} custom-call(bf16[25,48,1024]{2,1,0:T(8,128)(2,1)S(1)} %bitcast.23, s32[1,1024]{1,0:T(1,128)S(1)} %fusion.src_ref), custom_call_target="tpu_custom_call" | custom-call | flops 2617245696 | bytes 5242880 | tf_op jit(solution)/shard_map/reorder/pallas_call | solution.py:42
  26.4 0.0 copy-start.2
  26.4 1.5 copy-done.2
  27.9 5.7 %all-to-all-start = ((bf16[16,624,128]{2,1,0:T(8,128)(2,1)}), bf16[16,624,128]{2,1,0:T(8,128)(2,1)S(1)}, u32[]{:S(2)}, u32[]{:S(2)}) async-start(bf16[16,624,128]{2,1,0:T(8,128)(2,1)} %copy-done.2), calls=%async_computation | async-start | bytes 5111808 | tf_op jit(solution)/shard_map/all_to_all | solution.py:143
  33.5 67.8 %all-gather.3.cloned.1.call-done = bf16[16,25,16,128]{3,2,1,0:T(8,128)(2,1)} async-done(((bf16[4,25,16,128]{3,2,1,0:T(8,128)(2,1)}), bf16[16,25,16,128]{3,2,1,0:T(8,128)(2,1)}) %all-gather.3.cloned.1.call-update) | async-done | bytes 1638416 | tf_op jit(solution)/shard_map/all_gather | solution.py:140
  101.3 2.9 %copy.21 = bf16[4,4,25,16,128]{4,3,2,0,1:T(8,128)(2,1)} copy(bf16[4,4,25,16,128]{4,3,2,1,0:T(8,128)(2,1)} %bitcast.24) | data formatting | bytes 3276800 | tf_op jit(solution)/shard_map/all_gather | solution.py:140
  104.2 1.9 collective-permute-start
  106.1 2.5 %slice_bitcast_fusion.1 = (bf16[4,25,16,128]{3,2,1,0:T(8,128)(2,1)}, bf16[4,25,16,128]{3,2,1,0:T(8,128)(2,1)}, bf16[4,25,16,128]{3,2,1,0:T(8,128)(2,1)}, bf16[4,25,16,128]{3,2,1,0:T(8,128)(2,1)S(1)}) fusion(bf16[4,4,25,16,128]{4,3,2,1,0:T(8,128)(2,1)} %bitcast.25), kind=kLoop, calls=%fused_computation.1 | loop fusion | bytes 3276800 | tf_op jit(solution)/shard_map/squeeze | solution.py:146
  108.6 1.3 collective-permute-done
  109.9 2.5 %slice_bitcast_fusion = (bf16[4,25,16,128]{3,2,1,0:T(8,128)(2,1)}, bf16[4,25,16,128]{3,2,1,0:T(8,128)(2,1)}, bf16[4,25,16,128]{3,2,1,0:T(8,128)(2,1)}, bf16[4,25,16,128]{3,2,1,0:T(8,128)(2,1)S(1)}) fusion(bf16[4,4,25,16,128]{4,3,2,0,1:T(8,128)(2,1)} %collective-permute-done), kind=kLoop, calls=%fused_computation | loop fusion | bytes 3276800 | tf_op jit(solution)/shard_map/squeeze | solution.py:146
  112.4 0.0 all-to-all-done.a_ref
  112.4 2.0 product.4
  114.5 7.2 %all-to-all-start.2 = ((f32[16,96,128]{2,1,0:T(8,128)}), f32[16,96,128]{2,1,0:T(8,128)S(1)}, u32[]{:S(2)}, u32[]{:S(2)}) async-start(f32[16,96,128]{2,1,0:T(8,128)} %product.4), calls=%async_computation.2 | async-start | bytes 1572864 | tf_op jit(solution)/shard_map/all_to_all | solution.py:147
  121.7 0.0 copy-start.7
  121.7 1.0 copy-done.7
  122.7 0.0 copy-start.8
  122.7 1.0 copy-done.8
  123.7 2.0 product.5
  125.7 8.3 %all-to-all-done.2.refs_0_ = f32[16,96,128]{2,1,0:T(8,128)S(1)} async-done(((f32[16,96,128]{2,1,0:T(8,128)}), f32[16,96,128]{2,1,0:T(8,128)S(1)}, u32[]{:S(2)}, u32[]{:S(2)}) %all-to-all-start.2) | async-done | bytes 786464 | tf_op jit(solution)/shard_map/all_to_all | solution.py:147
  134.1 0.0 copy-start
  134.1 6.5 %all-to-all-start.3 = ((f32[16,96,128]{2,1,0:T(8,128)}), f32[16,96,128]{2,1,0:T(8,128)}, u32[]{:S(2)}, u32[]{:S(2)}) async-start(f32[16,96,128]{2,1,0:T(8,128)} %product.5), calls=%async_computation.3 | async-start | bytes 1572864 | tf_op jit(solution)/shard_map/all_to_all | solution.py:147
  140.5 0.0 copy-start.5
  140.5 1.0 copy-done.5
  141.5 0.0 copy-start.6
  141.5 1.0 copy-done.6
  142.5 2.0 product.6
  144.6 0.0 copy-done
  144.6 7.3 %all-to-all-done.3.refs_1_ = f32[16,96,128]{2,1,0:T(8,128)} async-done(((f32[16,96,128]{2,1,0:T(8,128)}), f32[16,96,128]{2,1,0:T(8,128)}, u32[]{:S(2)}, u32[]{:S(2)}) %all-to-all-start.3) | async-done | bytes 786464 | tf_op jit(solution)/shard_map/all_to_all | solution.py:147
  151.9 6.5 %all-to-all-start.4 = ((f32[16,96,128]{2,1,0:T(8,128)}), f32[16,96,128]{2,1,0:T(8,128)}, u32[]{:S(2)}, u32[]{:S(2)}) async-start(f32[16,96,128]{2,1,0:T(8,128)} %product.6), calls=%async_computation.4 | async-start | bytes 1572864 | tf_op jit(solution)/shard_map/all_to_all | solution.py:147
  158.4 0.0 copy-start.3
  158.4 1.0 copy-done.3
  159.4 0.0 copy-start.4
  159.4 1.0 copy-done.4
  160.4 1.1 product.7
  161.6 0.0 copy-start.1
  161.6 7.3 %all-to-all-done.4.refs_2_ = f32[16,96,128]{2,1,0:T(8,128)} async-done(((f32[16,96,128]{2,1,0:T(8,128)}), f32[16,96,128]{2,1,0:T(8,128)}, u32[]{:S(2)}, u32[]{:S(2)}) %all-to-all-start.4) | async-done | bytes 786464 | tf_op jit(solution)/shard_map/all_to_all | solution.py:147
  168.9 15.0 %all_to_all.36.refs_3_ = f32[16,96,128]{2,1,0:T(8,128)S(1)} all-to-all(f32[16,96,128]{2,1,0:T(8,128)S(1)} %product.7), channel_id=1, replica_groups=mesh['y'=4,'core'=2,'zh'=4,'x'=4,'zl'=4] {'y','x'}, dimensions={0} | all-to-all | bytes 1572864 | tf_op jit(solution)/shard_map/all_to_all | solution.py:147
  183.8 0.0 copy-done.1
  183.9 1.6 first_sum.1
  185.4 22.5 %all_to_all.37.in_ref = f32[16,32,128]{2,1,0:T(8,128)S(1)} all-to-all(f32[16,32,128]{2,1,0:T(8,128)S(1)} %first_sum.1), channel_id=1, replica_groups=mesh['y'=4,'core'=2,'zh'=4,'x'=4,'zl'=4] {'zh','zl'}, dimensions={0} | all-to-all | bytes 524288 | tf_op jit(solution)/shard_map/all_to_all | solution.py:148
  207.9 0.7 last_sum.1
  (1 shorter events, 0.0 us)
Async XLA Ops:
  6.5 94.8 %all-gather.3.cloned.1.call-start = ((), (), s32[]{:S(2)}) async-start(), calls=%async_computation.7 | async-start | bytes 2048000 | tf_op jit(solution)/shard_map/all_gather | solution.py:140
  21.7 1.7 copy-start.9
  26.4 1.5 copy-start.2
  27.9 84.6 %all-to-all-start = ((bf16[16,624,128]{2,1,0:T(8,128)(2,1)}), bf16[16,624,128]{2,1,0:T(8,128)(2,1)S(1)}, u32[]{:S(2)}, u32[]{:S(2)}) async-start(bf16[16,624,128]{2,1,0:T(8,128)(2,1)} %copy-done.2), calls=%async_computation | async-start | bytes 5111808 | tf_op jit(solution)/shard_map/all_to_all | solution.py:143
  104.2 5.7 %collective-permute-start = (bf16[4,4,25,16,128]{4,3,2,0,1:T(8,128)(2,1)}, bf16[4,4,25,16,128]{4,3,2,0,1:T(8,128)(2,1)}, u32[]{:S(2)}, u32[]{:S(2)}) collective-permute-start(bf16[4,4,25,16,128]{4,3,2,0,1:T(8,128)(2,1)} %copy.21), channel_id=1, source_target_pairs={{0,64},{64,0},{1,65},{65,1},{2,66},{66,2},{3,67},{67,3},{4,68},{68... | collective-permute-start | bytes 4915208 | tf_op jit(solution)/shard_map/ppermute | solution.py:145
  114.5 19.6 %all-to-all-start.2 = ((f32[16,96,128]{2,1,0:T(8,128)}), f32[16,96,128]{2,1,0:T(8,128)S(1)}, u32[]{:S(2)}, u32[]{:S(2)}) async-start(f32[16,96,128]{2,1,0:T(8,128)} %product.4), calls=%async_computation.2 | async-start | bytes 1572864 | tf_op jit(solution)/shard_map/all_to_all | solution.py:147
  121.7 1.0 copy-start.7
  122.7 1.0 copy-start.8
  134.1 10.5 %copy-start = (f32[16,96,128]{2,1,0:T(8,128)}, f32[16,96,128]{2,1,0:T(8,128)S(1)}, u32[]{:S(2)}) copy-start(f32[16,96,128]{2,1,0:T(8,128)S(1)} %all-to-all-done.2.refs_0_) | copy-start | bytes 2359300
  134.1 17.8 %all-to-all-start.3 = ((f32[16,96,128]{2,1,0:T(8,128)}), f32[16,96,128]{2,1,0:T(8,128)}, u32[]{:S(2)}, u32[]{:S(2)}) async-start(f32[16,96,128]{2,1,0:T(8,128)} %product.5), calls=%async_computation.3 | async-start | bytes 1572864 | tf_op jit(solution)/shard_map/all_to_all | solution.py:147
  140.5 1.0 copy-start.5
  141.5 1.0 copy-start.6
  151.9 17.0 %all-to-all-start.4 = ((f32[16,96,128]{2,1,0:T(8,128)}), f32[16,96,128]{2,1,0:T(8,128)}, u32[]{:S(2)}, u32[]{:S(2)}) async-start(f32[16,96,128]{2,1,0:T(8,128)} %product.6), calls=%async_computation.4 | async-start | bytes 1572864 | tf_op jit(solution)/shard_map/all_to_all | solution.py:147
  158.4 1.0 copy-start.3
  159.4 1.0 copy-start.4
  161.6 22.3 %copy-start.1 = (f32[16,96,128]{2,1,0:T(8,128)S(1)}, f32[16,96,128]{2,1,0:T(8,128)}, u32[]{:S(2)}) copy-start(f32[16,96,128]{2,1,0:T(8,128)} %copy-done) | copy-start | bytes 2359300
Sparse Core Ops, SparseCore 0:
  21.8 79.4 all-gather.2

commit v2 on v1

--- a/solution.py
+++ b/solution.py
@@ -51,44 +51,44 @@
     )(planes, src)
 
 
-def product_kernel(core_ref, a_ref, own_ref, other_ref, out_ref, right_ref):
-    core = core_ref[0]
-    mine = pl.ds(pl.multiple_of(core * 128, 128), 128)
-    theirs = pl.ds(pl.multiple_of((1 - core) * 128, 128), 128)
-    for k in range(K):
-        for zh in range(4):
-            rows = pl.ds(k * 64 + zh * 16, 16)
-            right_ref[rows, mine] = own_ref[zh, k]
-            right_ref[rows, theirs] = other_ref[zh, k]
-    right_ref[pl.ds(K * 64, 64), :] = jnp.zeros((64, 256), BF16)
+def product_kernel(place_ref, a_ref, *refs):
+    out_ref, right_ref = refs[-2:]
+    core = place_ref[0]
+    for near_ref, far_ref, whose in ((refs[0], refs[1], core), (refs[2], refs[3], 1 - core)):
+        for j in range(4):
+            lanes = pl.ds(pl.multiple_of(j * 256 + whose * 128, 128), 128)
+            for k in range(K):
+                for step, piece in ((0, near_ref[0, j, k]), (3, near_ref[1, j, k]),
+                                    (1, near_ref[2, j, k]), (2, far_ref[j, k])):
+                    right_ref[pl.ds(k * 64 + step * 16, 16), lanes] = piece
+    right_ref[pl.ds(K * 64, 64), :] = jnp.zeros((64, 1024), BF16)
     for y in range(4):
         left = jnp.concatenate(
             [a_ref[4 * y:4 * y + 4, p * ROWS:(p + 1) * ROWS, :].reshape(192, 128) for p in range(PAIRS)], axis=1
         )
         block = jnp.dot(left, right_ref[...], preferred_element_type=F32)
         for x in range(4):
-            part = block[:, x * 64:(x + 1) * 64]
-            out_ref[y * 4 + x] = jnp.concatenate([part[:96], part[96:]], axis=1)
+            for j in range(4):
+                part = block[:, j * 256 + x * 64:j * 256 + (x + 1) * 64]
+                out_ref[y * 4 + x, j * 96:(j + 1) * 96] = jnp.concatenate([part[:96], part[96:]], axis=1)
 
 
-def product(core, a, own, other):
+def product(place, a, near, far, near_other, far_other):
     return pl.pallas_call(
         product_kernel,
-        out_shape=jax.ShapeDtypeStruct((16, 96, 128), F32),
-        in_specs=[SMEM, VMEM, VMEM, VMEM],
+        out_shape=jax.ShapeDtypeStruct((16, 384, 128), F32),
+        in_specs=[SMEM] + [VMEM] * 5,
         out_specs=VMEM,
-        scratch_shapes=[pltpu.VMEM((DEPTH, 256), BF16)],
+        scratch_shapes=[pltpu.VMEM((DEPTH, 1024), BF16)],
         compiler_params=params(),
-        cost_estimate=pl.CostEstimate(flops=2 * 768 * DEPTH * 256, bytes_accessed=5 * 2**20, transcendentals=0),
+        cost_estimate=pl.CostEstimate(flops=2 * 768 * DEPTH * 1024, bytes_accessed=11 * 2**20, transcendentals=0),
         name="product",
-    )(core, a, own, other)
+    )(place, a, near, far, near_other, far_other)
 
 
-def first_sum_kernel(*refs):
-    out_ref = refs[-1]
+def pack_kernel(in_ref, out_ref):
     for zh in range(4):
-        total = jnp.sum(refs[zh][...], axis=0)
-        turned = total.T
+        turned = in_ref[zh * 96:(zh + 1) * 96].T
         for zl in range(4):
             at = zl * 16
             out_ref[zh * 4 + zl, :16, :96] = turned[at:at + 16]
@@ -96,16 +96,16 @@
             out_ref[zh * 4 + zl, :, 96:] = jnp.zeros((32, 32), F32)
 
 
-def first_sum(parts):
+def pack(total):
     return pl.pallas_call(
-        first_sum_kernel,
+        pack_kernel,
         out_shape=jax.ShapeDtypeStruct((16, 32, 128), F32),
-        in_specs=[VMEM] * 4,
+        in_specs=[VMEM],
         out_specs=VMEM,
         compiler_params=params(),
-        cost_estimate=pl.CostEstimate(flops=2**20, bytes_accessed=4 * 2**20, transcendentals=0),
-        name="first_sum",
-    )(*parts)
+        cost_estimate=pl.CostEstimate(flops=2**16, bytes_accessed=2**19, transcendentals=0),
+        name="pack",
+    )(total)
 
 
 def last_sum_kernel(in_ref, out_ref):
@@ -127,25 +127,35 @@
     )(parts)
 
 
-def source_of_lane():
+def source_of_lane(zh):
     lane = jnp.arange(1024, dtype=jnp.int32)
-    y, xb, parity, zh, i = lane // 256, lane // 128 % 2, lane // 64 % 2, lane // 16 % 4, lane % 16
-    return (parity * 512 + zh * 128 + xb * 64 + y * 16 + i).reshape(1, 1024)
+    y, xb, parity, step, i = lane // 256, lane // 128 % 2, lane // 64 % 2, lane // 16 % 4, lane % 16
+    return (parity * 512 + (step + zh) % 4 * 128 + xb * 64 + y * 16 + i).reshape(1, 1024)
+
+
+def shift(value, axis, by):
+    return lax.ppermute(value, axis, [(i, (i + by) % 4) for i in range(4)])
+
+
+def swap(value):
+    return lax.ppermute(value, "core", [(0, 1), (1, 0)])
 
 
 def local(amplitudes, integrals):
-    core = lax.axis_index("core").astype(jnp.int32).reshape(1)
+    core, zh = (lax.axis_index(a).astype(jnp.int32) for a in ("core", "zh"))
+    place = core.reshape(1)
     by_y = integrals.reshape(K, 4, 16, 128).transpose(1, 0, 2, 3)
-    blocks = lax.all_to_all(by_y, "y", 0, 0, tiled=True)
-    gathered = lax.all_gather(blocks, "zh", axis=0, tiled=False)
-
-    sent = reorder(amplitudes.transpose(1, 0, 2), source_of_lane())
+    own = lax.all_to_all(by_y, "y", 0, 0, tiled=True)
+    sent = reorder(amplitudes.transpose(1, 0, 2), source_of_lane(zh))
     rows = lax.all_to_all(sent, ("y", "x"), 0, 0, tiled=True)
 
-    swapped = lax.ppermute(gathered, "core", [(0, 1), (1, 0)])
-    partial = [product(core, rows, gathered[:, c], swapped[:, c]) for c in range(4)]
-    arrived = [lax.all_to_all(part, ("y", "x"), 0, 0, tiled=True) for part in partial]
-    final = lax.all_to_all(first_sum(arrived), ("zh", "zl"), 0, 0, tiled=True)
+    below, above = shift(own, "zh", 1), shift(own, "zh", -1)
+    near = jnp.stack([own, below, above])
+    far = jnp.concatenate([shift(below[:, :13], "zh", 1), shift(above[:, 13:], "zh", -1)], axis=1)
+    part = product(place, rows, near, far, swap(near), swap(far))
+    arrived = lax.all_to_all(part, ("y", "x"), 0, 0, tiled=True)
+    total = jnp.sum(arrived, axis=0)
+    final = lax.all_to_all(pack(total), ("zh", "zl"), 0, 0, tiled=True)
     return last_sum(final).T
 
 

time: 218 us -> 186 us (0.85)
  waiting for transfers between devices: 91.9 us -> 47.5 us
  blocking collectives: 51.5 us -> 78.7 us
  local copies, waits for them, and re-layouts: 18.2 us -> 3.56 us
  between operations: 13.5 us -> 0.11 us
  starting transfers between devices: 27.8 us -> 40.6 us
    all_gather x1 -> x0, waiting for transfers between devices: 67.8 us -> none  [local(): gathered = lax.all_gather(blocks, 'zh', axis=0, tiled=False)]
    ppermute x1 -> x6, waiting for transfers between devices: 1.26 us -> 47.5 us  [the longest x4 45.8 us: shift(): return lax.ppermute(value, axis, [(i, (i + by) % 4) for i in range(4)])]
    all_to_all x3 -> x2, blocking collectives: 51.5 us -> 78.7 us  [the longest x1 44.7 us: local(): arrived = lax.all_to_all(part, ('y', 'x'), 0, 0, tiled=True)]
    ppermute x1 -> x6, starting transfers between devices: 1.91 us -> 26.7 us  [the longest x4 22.9 us: shift(): return lax.ppermute(value, axis, [(i, (i + by) % 4) for i in range(4)])]
    all_to_all x3 -> x1, waiting for transfers between devices: 22.9 us -> 0.01 us  [local(): own = lax.all_to_all(by_y, 'y', 0, 0, tiled=True)]
    all_to_all x3 -> x1, starting transfers between devices: 20.2 us -> 9.03 us  [local(): own = lax.all_to_all(by_y, 'y', 0, 0, tiled=True)]
    unnamed x20 -> x3, local copies, waits for them, and re-layouts: 9.16 us -> 1.7 us
    squeeze x2 -> x0, local copies, waits for them, and re-layouts: 5.09 us -> none  [the longest x1 2.55 us: local(): gathered[:, c]]
  transfers between devices with their start and end apart: 6 -> 8, of which waited for: 5 -> 4; matrix products, arithmetic and copies ran while one was open for 4% -> 1% of each run, Pallas kernels for 4% -> 2%
where the time goes in v2:
time: 186 us; the launch traced here: 183 us
  blocking collectives  78.7 us (42%)
  waiting for transfers between devices  47.5 us (26%)
  starting transfers between devices  40.6 us (22%)
  Pallas kernels  11 us (6%)
  local copies, waits for them, and re-layouts  3.56 us (2%)
    ppermute x4, waiting for transfers between devices, shift(): return lax.ppermute(value, axis, [(i, (i + by) % 4) for i in range(4)])  45.8 us
    all_to_all x1, blocking collectives, local(): arrived = lax.all_to_all(part, ('y', 'x'), 0, 0, tiled=True)  44.7 us
    all_to_all x1, blocking collectives, local(): final = lax.all_to_all(pack(total), ('zh', 'zl'), 0, 0, tiled=True)  34.1 us
    ppermute x4, starting transfers between devices, shift(): return lax.ppermute(value, axis, [(i, (i + by) % 4) for i in range(4)])  22.9 us
    all_to_all x1, starting transfers between devices, local(): own = lax.all_to_all(by_y, 'y', 0, 0, tiled=True)  9.03 us
    pallas_call x1, Pallas kernels, product(): pl.pallas_call(product_kernel, out_shape=jax.ShapeDtypeStruct((16, 384, 1...  5.73 us
    all_to_all x1, starting transfers between devices, local(): rows = lax.all_to_all(sent, ('y', 'x'), 0, 0, tiled=True)  4.86 us
    pallas_call x1, Pallas kernels, reorder(): pl.pallas_call(reorder_kernel, out_shape=jax.ShapeDtypeStruct((16, PAIRS...  4.45 us
  transfers between devices with their start and end apart: 8, of which 4 were waited for; matrix products, arithmetic and copies ran while one was open for 1% of the time, Pallas kernels for 2%

profile of v2, /device:TPU:24, one launch (start us, length us, event | category | flops | bytes accessed | tf_op | source)
XLA Modules:
  0.0 182.9 jit_solution(6749733644495662217)
XLA Ops:
  0.0 1.8 copy.5
  1.8 9.0 %all-to-all-start.1 = ((bf16[4,25,16,128]{3,2,1,0:T(8,128)(2,1)}), bf16[4,25,16,128]{3,2,1,0:T(8,128)(2,1)S(1)}, u32[]{:S(2)}, u32[]{:S(2)}) async-start(bf16[4,25,16,128]{3,2,1,0:T(8,128)(2,1)} %bitcast.9), calls=%async_computation.1 | async-start | bytes 819200 | tf_op jit(solution)/shard_map/all_to_all | solution.py:148
  10.9 0.0 copy-start
  10.9 1.7 copy-done
  12.6 4.5 %reorder.1 = bf16[16,624,128]{2,1,0:T(8,128)(2,1)} custom-call(bf16[25,48,1024]{2,1,0:T(8,128)(2,1)S(1)} %bitcast.10, s32[1,1024]{1,0:T(1,128)S(1)} %fusion.src_ref), custom_call_target="tpu_custom_call" | custom-call | flops 2617245696 | bytes 5242880 | tf_op jit(solution)/shard_map/reorder/pallas_call | solution.py:42
  17.0 0.0 all-to-all-done.1
  17.0 4.9 %all-to-all-start = ((bf16[16,624,128]{2,1,0:T(8,128)(2,1)}), bf16[16,624,128]{2,1,0:T(8,128)(2,1)S(1)}, u32[]{:S(2)}, u32[]{:S(2)}) async-start(bf16[16,624,128]{2,1,0:T(8,128)(2,1)} %reorder.1), calls=%async_computation | async-start | bytes 5111808 | tf_op jit(solution)/shard_map/all_to_all | solution.py:150
  21.9 10.8 %collective-permute-start.1 = (bf16[4,25,16,128]{3,2,1,0:T(8,128)(2,1)S(1)}, bf16[4,25,16,128]{3,2,1,0:T(8,128)(2,1)S(1)}, u32[]{:S(2)}, u32[]{:S(2)}) collective-permute-start(bf16[4,25,16,128]{3,2,1,0:T(8,128)(2,1)S(1)} %all-to-all-done.1), channel_id=1, source_target_pairs={{0,48},{16,0},{32,16},{48,32},{1,49},{17,1},{33,17},{49,33},{2,50}... | collective-permute-start | bytes 1228808 | tf_op jit(solution)/shard_map/ppermute | solution.py:137
  32.7 1.9 %collective-permute-start = (bf16[4,25,16,128]{3,2,1,0:T(8,128)(2,1)S(1)}, bf16[4,25,16,128]{3,2,1,0:T(8,128)(2,1)S(1)}, u32[]{:S(2)}, u32[]{:S(2)}) collective-permute-start(bf16[4,25,16,128]{3,2,1,0:T(8,128)(2,1)S(1)} %all-to-all-done.1), channel_id=1, source_target_pairs={{0,16},{16,32},{32,48},{48,0},{1,17},{17,33},{33,49},{49,1},{2,18}... | collective-permute-start | bytes 1228808 | tf_op jit(solution)/shard_map/ppermute | solution.py:137
  34.6 32.1 %collective-permute-done.1 = bf16[4,25,16,128]{3,2,1,0:T(8,128)(2,1)S(1)} collective-permute-done((bf16[4,25,16,128]{3,2,1,0:T(8,128)(2,1)S(1)}, bf16[4,25,16,128]{3,2,1,0:T(8,128)(2,1)S(1)}, u32[]{:S(2)}, u32[]{:S(2)}) %collective-permute-start.1) | collective-permute-done | bytes 409632 | tf_op jit(solution)/shard_map/ppermute | solution.py:137
  66.7 0.0 collective-permute-done
  66.7 1.2 pad_maximum_fusion.refs_0_
  67.9 1.9 %collective-permute-start.4 = (bf16[3,4,25,16,128]{4,3,2,1,0:T(8,128)(2,1)}, bf16[3,4,25,16,128]{4,3,2,1,0:T(8,128)(2,1)}, u32[]{:S(2)}, u32[]{:S(2)}) collective-permute-start(bf16[3,4,25,16,128]{4,3,2,1,0:T(8,128)(2,1)} %pad_maximum_fusion.refs_0_), channel_id=1, source_target_pairs={{0,64},{64,0},{1,65},{65,1},{2,66},{66,2},{3,67},{67,3},{4,68},{68... | collective-permute-start | bytes 3686408 | tf_op jit(solution)/shard_map/ppermute | solution.py:141
  69.8 6.1 %collective-permute-start.2 = (bf16[4,13,16,128]{3,2,1,0:T(8,128)(2,1)S(1)}, bf16[4,13,16,128]{3,2,1,0:T(8,128)(2,1)S(1)}, u32[]{:S(2)}, u32[]{:S(2)}) collective-permute-start(bf16[4,13,16,128]{3,2,1,0:T(8,128)(2,1)S(1)} %slice.8), channel_id=1, source_target_pairs={{0,16},{16,32},{32,48},{48,0},{1,17},{17,33},{33,49},{49,1},{2,18}... | collective-permute-start | bytes 638984 | tf_op jit(solution)/shard_map/ppermute | solution.py:137
  76.0 4.1 %collective-permute-start.3 = (bf16[4,12,16,128]{3,2,1,0:T(8,128)(2,1)S(1)}, bf16[4,12,16,128]{3,2,1,0:T(8,128)(2,1)S(1)}, u32[]{:S(2)}, u32[]{:S(2)}) collective-permute-start(bf16[4,12,16,128]{3,2,1,0:T(8,128)(2,1)S(1)} %slice.9), channel_id=1, source_target_pairs={{0,48},{16,0},{32,16},{48,32},{1,49},{17,1},{33,17},{49,33},{2,50}... | collective-permute-start | bytes 589832 | tf_op jit(solution)/shard_map/ppermute | solution.py:137
  80.1 4.1 %collective-permute-done.2 = bf16[4,13,16,128]{3,2,1,0:T(8,128)(2,1)S(1)} collective-permute-done((bf16[4,13,16,128]{3,2,1,0:T(8,128)(2,1)S(1)}, bf16[4,13,16,128]{3,2,1,0:T(8,128)(2,1)S(1)}, u32[]{:S(2)}, u32[]{:S(2)}) %collective-permute-start.2) | collective-permute-done | bytes 213024 | tf_op jit(solution)/shard_map/ppermute | solution.py:137
  84.1 9.7 %collective-permute-done.3 = bf16[4,12,16,128]{3,2,1,0:T(8,128)(2,1)S(1)} collective-permute-done((bf16[4,12,16,128]{3,2,1,0:T(8,128)(2,1)S(1)}, bf16[4,12,16,128]{3,2,1,0:T(8,128)(2,1)S(1)}, u32[]{:S(2)}, u32[]{:S(2)}) %collective-permute-start.3) | collective-permute-done | bytes 196640 | tf_op jit(solution)/shard_map/ppermute | solution.py:137
  93.8 1.9 %collective-permute-start.5 = (bf16[4,25,16,128]{3,2,1,0:T(8,128)(2,1)S(1)}, bf16[4,25,16,128]{3,2,1,0:T(8,128)(2,1)S(1)}, u32[]{:S(2)}, u32[]{:S(2)}) collective-permute-start(bf16[4,25,16,128]{3,2,1,0:T(8,128)(2,1)S(1)} %constant_dynamic-update-slice_fusion.refs_1_), channel_id=1, source_target_pairs={{0,64},{64,0},{1,65},{65,1},{2,66},{66,2},{3,67},{67,3},{4,68},{68... | collective-permute-start | bytes 1228808 | tf_op jit(solution)/shard_map/ppermute | solution.py:141
  95.8 1.7 collective-permute-done.5.refs_3_
  97.5 0.0 collective-permute-done.4.refs_2_
  97.5 0.0 all-to-all-done.a_ref
  97.5 5.7 %product.1 = f32[16,384,128]{2,1,0:T(8,128)S(1)} custom-call(s32[1]{0:T(128)} %bitcast.place_ref, bf16[16,624,128]{2,1,0:T(8,128)(2,1)S(1)} %all-to-all-done.a_ref, bf16[3,4,25,16,128]{4,3,2,1,0:T(8,128)(2,1)} %pad_maximum_fusion.refs_0_, bf16[4,25,16,128]{3,2,1,0:T(8,128)(2,1)S(1)} %constant_dynamic-update-slice_fusion.refs_1_, ...), custom_call_target="tpu_custom_call" | custom-call | flops 2617245696 | bytes 11534336 | tf_op jit(solution)/shard_map/product/pallas_call | solution.py:77
  103.2 44.7 %all_to_all.20 = f32[16,384,128]{2,1,0:T(8,128)S(1)} all-to-all(f32[16,384,128]{2,1,0:T(8,128)S(1)} %product.1), channel_id=1, replica_groups=mesh['y'=4,'core'=2,'zh'=4,'x'=4,'zl'=4] {'y','x'}, dimensions={0} | all-to-all | bytes 6291456 | tf_op jit(solution)/shard_map/all_to_all | solution.py:156
  147.9 0.2 reduce_sum.9.in_ref
  148.0 0.1 pack.1
  148.2 34.1 %all_to_all.21.in_ref = f32[16,32,128]{2,1,0:T(8,128)S(1)} all-to-all(f32[16,32,128]{2,1,0:T(8,128)S(1)} %pack.1), channel_id=1, replica_groups=mesh['y'=4,'core'=2,'zh'=4,'x'=4,'zl'=4] {'zh','zl'}, dimensions={0} | all-to-all | bytes 524288 | tf_op jit(solution)/shard_map/all_to_all | solution.py:158
  182.2 0.7 last_sum.1
  (5 shorter events, 0.1 us)
Async XLA Ops:
  1.8 15.2 %all-to-all-start.1 = ((bf16[4,25,16,128]{3,2,1,0:T(8,128)(2,1)}), bf16[4,25,16,128]{3,2,1,0:T(8,128)(2,1)S(1)}, u32[]{:S(2)}, u32[]{:S(2)}) async-start(bf16[4,25,16,128]{3,2,1,0:T(8,128)(2,1)} %bitcast.9), calls=%async_computation.1 | async-start | bytes 819200 | tf_op jit(solution)/shard_map/all_to_all | solution.py:148
  10.9 1.7 copy-start
  17.0 80.5 %all-to-all-start = ((bf16[16,624,128]{2,1,0:T(8,128)(2,1)}), bf16[16,624,128]{2,1,0:T(8,128)(2,1)S(1)}, u32[]{:S(2)}, u32[]{:S(2)}) async-start(bf16[16,624,128]{2,1,0:T(8,128)(2,1)} %reorder.1), calls=%async_computation | async-start | bytes 5111808 | tf_op jit(solution)/shard_map/all_to_all | solution.py:150
  21.9 44.8 %collective-permute-start.1 = (bf16[4,25,16,128]{3,2,1,0:T(8,128)(2,1)S(1)}, bf16[4,25,16,128]{3,2,1,0:T(8,128)(2,1)S(1)}, u32[]{:S(2)}, u32[]{:S(2)}) collective-permute-start(bf16[4,25,16,128]{3,2,1,0:T(8,128)(2,1)S(1)} %all-to-all-done.1), channel_id=1, source_target_pairs={{0,48},{16,0},{32,16},{48,32},{1,49},{17,1},{33,17},{49,33},{2,50}... | collective-permute-start | bytes 1228808 | tf_op jit(solution)/shard_map/ppermute | solution.py:137
  32.7 34.0 %collective-permute-start = (bf16[4,25,16,128]{3,2,1,0:T(8,128)(2,1)S(1)}, bf16[4,25,16,128]{3,2,1,0:T(8,128)(2,1)S(1)}, u32[]{:S(2)}, u32[]{:S(2)}) collective-permute-start(bf16[4,25,16,128]{3,2,1,0:T(8,128)(2,1)S(1)} %all-to-all-done.1), channel_id=1, source_target_pairs={{0,16},{16,32},{32,48},{48,0},{1,17},{17,33},{33,49},{49,1},{2,18}... | collective-permute-start | bytes 1228808 | tf_op jit(solution)/shard_map/ppermute | solution.py:137
  67.9 29.6 %collective-permute-start.4 = (bf16[3,4,25,16,128]{4,3,2,1,0:T(8,128)(2,1)}, bf16[3,4,25,16,128]{4,3,2,1,0:T(8,128)(2,1)}, u32[]{:S(2)}, u32[]{:S(2)}) collective-permute-start(bf16[3,4,25,16,128]{4,3,2,1,0:T(8,128)(2,1)} %pad_maximum_fusion.refs_0_), channel_id=1, source_target_pairs={{0,64},{64,0},{1,65},{65,1},{2,66},{66,2},{3,67},{67,3},{4,68},{68... | collective-permute-start | bytes 3686408 | tf_op jit(solution)/shard_map/ppermute | solution.py:141
  69.8 14.3 %collective-permute-start.2 = (bf16[4,13,16,128]{3,2,1,0:T(8,128)(2,1)S(1)}, bf16[4,13,16,128]{3,2,1,0:T(8,128)(2,1)S(1)}, u32[]{:S(2)}, u32[]{:S(2)}) collective-permute-start(bf16[4,13,16,128]{3,2,1,0:T(8,128)(2,1)S(1)} %slice.8), channel_id=1, source_target_pairs={{0,16},{16,32},{32,48},{48,0},{1,17},{17,33},{33,49},{49,1},{2,18}... | collective-permute-start | bytes 638984 | tf_op jit(solution)/shard_map/ppermute | solution.py:137
  76.0 17.8 %collective-permute-start.3 = (bf16[4,12,16,128]{3,2,1,0:T(8,128)(2,1)S(1)}, bf16[4,12,16,128]{3,2,1,0:T(8,128)(2,1)S(1)}, u32[]{:S(2)}, u32[]{:S(2)}) collective-permute-start(bf16[4,12,16,128]{3,2,1,0:T(8,128)(2,1)S(1)} %slice.9), channel_id=1, source_target_pairs={{0,48},{16,0},{32,16},{48,32},{1,49},{17,1},{33,17},{49,33},{2,50}... | collective-permute-start | bytes 589832 | tf_op jit(solution)/shard_map/ppermute | solution.py:137
  93.8 3.6 %collective-permute-start.5 = (bf16[4,25,16,128]{3,2,1,0:T(8,128)(2,1)S(1)}, bf16[4,25,16,128]{3,2,1,0:T(8,128)(2,1)S(1)}, u32[]{:S(2)}, u32[]{:S(2)}) collective-permute-start(bf16[4,25,16,128]{3,2,1,0:T(8,128)(2,1)S(1)} %constant_dynamic-update-slice_fusion.refs_1_), channel_id=1, source_target_pairs={{0,64},{64,0},{1,65},{65,1},{2,66},{66,2},{3,67},{67,3},{4,68},{68... | collective-permute-start | bytes 1228808 | tf_op jit(solution)/shard_map/ppermute | solution.py:141

commit v3 on v2

--- a/solution.py
+++ b/solution.py
@@ -67,16 +67,21 @@
             [a_ref[4 * y:4 * y + 4, p * ROWS:(p + 1) * ROWS, :].reshape(192, 128) for p in range(PAIRS)], axis=1
         )
         block = jnp.dot(left, right_ref[...], preferred_element_type=F32)
+        largest = jnp.max(jnp.max(jnp.abs(block), axis=0, keepdims=True), axis=1, keepdims=True)
+        exponent = jnp.ceil(jnp.log2(jnp.maximum(largest, 2.0 ** -100)))
+        block = block * jnp.exp2(7.0 - exponent)
+        block = block * jnp.abs(block)
         for x in range(4):
             for j in range(4):
                 part = block[:, j * 256 + x * 64:j * 256 + (x + 1) * 64]
                 out_ref[y * 4 + x, j * 96:(j + 1) * 96] = jnp.concatenate([part[:96], part[96:]], axis=1)
+            out_ref[y * 4 + x, 384:] = jnp.broadcast_to(exponent, (16, 128))
 
 
 def product(place, a, near, far, near_other, far_other):
     return pl.pallas_call(
         product_kernel,
-        out_shape=jax.ShapeDtypeStruct((16, 384, 128), F32),
+        out_shape=jax.ShapeDtypeStruct((16, 400, 128), F32),
         in_specs=[SMEM] + [VMEM] * 5,
         out_specs=VMEM,
         scratch_shapes=[pltpu.VMEM((DEPTH, 1024), BF16)],
@@ -152,9 +157,12 @@
     below, above = shift(own, "zh", 1), shift(own, "zh", -1)
     near = jnp.stack([own, below, above])
     far = jnp.concatenate([shift(below[:, :13], "zh", 1), shift(above[:, 13:], "zh", -1)], axis=1)
-    part = product(place, rows, near, far, swap(near), swap(far))
-    arrived = lax.all_to_all(part, ("y", "x"), 0, 0, tiled=True)
-    total = jnp.sum(arrived, axis=0)
+    part = product(place, rows, near, far, swap(near), swap(far)).astype(jnp.float16)
+    arrived = lax.all_to_all(part, ("y", "x"), 0, 0, tiled=True).astype(F32)
+    scale = jnp.exp2(arrived[:, 384:385, :1] - 7.0)
+    coded = arrived[:, :384]
+    root = jnp.sqrt(jnp.abs(coded)) * scale
+    total = jnp.sum(jnp.where(coded < 0, -root, root), axis=0)
     final = lax.all_to_all(pack(total), ("zh", "zl"), 0, 0, tiled=True)
     return last_sum(final).T
 

time: 186 us -> 170 us (0.914)
  blocking collectives: 78.7 us -> 62.9 us
  waiting for transfers between devices: 47.5 us -> 45.2 us
    all_to_all x1, blocking collectives: 44.7 us -> 28.8 us  [local(): arrived = lax.all_to_all(part, ('y', 'x'), 0, 0, tiled=True).astype(F32)]
    ppermute x4, waiting for transfers between devices: 45.8 us -> 43.5 us  [shift(): return lax.ppermute(value, axis, [(i, (i + by) % 4) for i in range(4)])]
  transfers between devices with their start and end apart: 8 -> 8, of which waited for: 4 -> 4; matrix products, arithmetic and copies ran while one was open for 1% -> 1% of each run, Pallas kernels for 2% -> 3%
where the time goes in v3:
time: 170 us; the launch traced here: 167 us
  blocking collectives  62.9 us (37%)
  waiting for transfers between devices  45.2 us (27%)
  starting transfers between devices  40.6 us (24%)
  Pallas kernels  11.5 us (7%)
  local copies, waits for them, and re-layouts  3.55 us (2%)
  other arithmetic  3.21 us (2%)
    ppermute x4, waiting for transfers between devices, shift(): return lax.ppermute(value, axis, [(i, (i + by) % 4) for i in range(4)])  43.5 us
    all_to_all x1, blocking collectives, local(): final = lax.all_to_all(pack(total), ('zh', 'zl'), 0, 0, tiled=True)  34.1 us
    all_to_all x1, blocking collectives, local(): arrived = lax.all_to_all(part, ('y', 'x'), 0, 0, tiled=True).astype(F32)  28.8 us
    ppermute x4, starting transfers between devices, shift(): return lax.ppermute(value, axis, [(i, (i + by) % 4) for i in range(4)])  22.9 us
    all_to_all x1, starting transfers between devices, local(): own = lax.all_to_all(by_y, 'y', 0, 0, tiled=True)  9.03 us
    pallas_call x1, Pallas kernels, product(): pl.pallas_call(product_kernel, out_shape=jax.ShapeDtypeStruct((16, 400, 1...  6.16 us
    all_to_all x1, starting transfers between devices, local(): rows = lax.all_to_all(sent, ('y', 'x'), 0, 0, tiled=True)  4.85 us
    pallas_call x1, Pallas kernels, reorder(): pl.pallas_call(reorder_kernel, out_shape=jax.ShapeDtypeStruct((16, PAIRS...  4.47 us
  transfers between devices with their start and end apart: 8, of which 4 were waited for; matrix products, arithmetic and copies ran while one was open for 1% of the time, Pallas kernels for 3%

profile of v3, /device:TPU:24, one launch (start us, length us, event | category | flops | bytes accessed | tf_op | source)
XLA Modules:
  0.0 167.1 jit_solution(6546196811963236796)
XLA Ops:
  0.0 1.8 %copy.5 = bf16[25,4,16,128]{3,2,0,1:T(8,128)(2,1)} copy(bf16[25,4,16,128]{3,2,1,0:T(8,128)(2,1)} %bitcast.14) | data formatting | bytes 819200 | tf_op jit(solution)/shard_map/reshape | solution.py:152
  1.8 9.0 %all-to-all-start.1 = ((bf16[4,25,16,128]{3,2,1,0:T(8,128)(2,1)}), bf16[4,25,16,128]{3,2,1,0:T(8,128)(2,1)S(1)}, u32[]{:S(2)}, u32[]{:S(2)}) async-start(bf16[4,25,16,128]{3,2,1,0:T(8,128)(2,1)} %bitcast.9), calls=%async_computation.1 | async-start | bytes 819200 | tf_op jit(solution)/shard_map/all_to_all | solution.py:153
  10.9 0.0 copy-start
  10.9 1.7 %copy-done = bf16[48,25,1024]{2,0,1:T(8,128)(2,1)S(1)} copy-done((bf16[48,25,1024]{2,0,1:T(8,128)(2,1)S(1)}, bf16[48,25,1024]{2,0,1:T(8,128)(2,1)}, u32[]{:S(2)}) %copy-start) | copy-done | bytes 2457624
  12.6 4.5 %reorder.1 = bf16[16,624,128]{2,1,0:T(8,128)(2,1)} custom-call(bf16[25,48,1024]{2,1,0:T(8,128)(2,1)S(1)} %bitcast.10, s32[1,1024]{1,0:T(1,128)S(1)} %fusion.4.src_ref), custom_call_target="tpu_custom_call" | custom-call | flops 2617245696 | bytes 5242880 | tf_op jit(solution)/shard_map/reorder/pallas_call | solution.py:42
  17.0 0.0 all-to-all-done.1
  17.0 4.8 %all-to-all-start = ((bf16[16,624,128]{2,1,0:T(8,128)(2,1)}), bf16[16,624,128]{2,1,0:T(8,128)(2,1)S(1)}, u32[]{:S(2)}, u32[]{:S(2)}) async-start(bf16[16,624,128]{2,1,0:T(8,128)(2,1)} %reorder.1), calls=%async_computation | async-start | bytes 5111808 | tf_op jit(solution)/shard_map/all_to_all | solution.py:155
  21.9 10.8 %collective-permute-start.1 = (bf16[4,25,16,128]{3,2,1,0:T(8,128)(2,1)S(1)}, bf16[4,25,16,128]{3,2,1,0:T(8,128)(2,1)S(1)}, u32[]{:S(2)}, u32[]{:S(2)}) collective-permute-start(bf16[4,25,16,128]{3,2,1,0:T(8,128)(2,1)S(1)} %all-to-all-done.1), channel_id=1, source_target_pairs={{0,48},{16,0},{32,16},{48,32},{1,49},{17,1},{33,17},{49,33},{2,50}... | collective-permute-start | bytes 1228808 | tf_op jit(solution)/shard_map/ppermute | solution.py:142
  32.7 1.9 %collective-permute-start = (bf16[4,25,16,128]{3,2,1,0:T(8,128)(2,1)S(1)}, bf16[4,25,16,128]{3,2,1,0:T(8,128)(2,1)S(1)}, u32[]{:S(2)}, u32[]{:S(2)}) collective-permute-start(bf16[4,25,16,128]{3,2,1,0:T(8,128)(2,1)S(1)} %all-to-all-done.1), channel_id=1, source_target_pairs={{0,16},{16,32},{32,48},{48,0},{1,17},{17,33},{33,49},{49,1},{2,18}... | collective-permute-start | bytes 1228808 | tf_op jit(solution)/shard_map/ppermute | solution.py:142
  34.6 32.1 %collective-permute-done.1 = bf16[4,25,16,128]{3,2,1,0:T(8,128)(2,1)S(1)} collective-permute-done((bf16[4,25,16,128]{3,2,1,0:T(8,128)(2,1)S(1)}, bf16[4,25,16,128]{3,2,1,0:T(8,128)(2,1)S(1)}, u32[]{:S(2)}, u32[]{:S(2)}) %collective-permute-start.1) | collective-permute-done | bytes 409632 | tf_op jit(solution)/shard_map/ppermute | solution.py:142
  66.7 0.0 collective-permute-done
  66.7 1.2 pad_maximum_fusion.refs_0_
  67.9 1.9 %collective-permute-start.4 = (bf16[3,4,25,16,128]{4,3,2,1,0:T(8,128)(2,1)}, bf16[3,4,25,16,128]{4,3,2,1,0:T(8,128)(2,1)}, u32[]{:S(2)}, u32[]{:S(2)}) collective-permute-start(bf16[3,4,25,16,128]{4,3,2,1,0:T(8,128)(2,1)} %pad_maximum_fusion.refs_0_), channel_id=1, source_target_pairs={{0,64},{64,0},{1,65},{65,1},{2,66},{66,2},{3,67},{67,3},{4,68},{68... | collective-permute-start | bytes 3686408 | tf_op jit(solution)/shard_map/ppermute | solution.py:146
  69.8 6.1 %collective-permute-start.2 = (bf16[4,13,16,128]{3,2,1,0:T(8,128)(2,1)S(1)}, bf16[4,13,16,128]{3,2,1,0:T(8,128)(2,1)S(1)}, u32[]{:S(2)}, u32[]{:S(2)}) collective-permute-start(bf16[4,13,16,128]{3,2,1,0:T(8,128)(2,1)S(1)} %slice.16), channel_id=1, source_target_pairs={{0,16},{16,32},{32,48},{48,0},{1,17},{17,33},{33,49},{49,1},{2,18}... | collective-permute-start | bytes 638984 | tf_op jit(solution)/shard_map/ppermute | solution.py:142
  76.0 4.1 %collective-permute-start.3 = (bf16[4,12,16,128]{3,2,1,0:T(8,128)(2,1)S(1)}, bf16[4,12,16,128]{3,2,1,0:T(8,128)(2,1)S(1)}, u32[]{:S(2)}, u32[]{:S(2)}) collective-permute-start(bf16[4,12,16,128]{3,2,1,0:T(8,128)(2,1)S(1)} %slice.17), channel_id=1, source_target_pairs={{0,48},{16,0},{32,16},{48,32},{1,49},{17,1},{33,17},{49,33},{2,50}... | collective-permute-start | bytes 589832 | tf_op jit(solution)/shard_map/ppermute | solution.py:142
  80.1 10.2 %collective-permute-done.2 = bf16[4,13,16,128]{3,2,1,0:T(8,128)(2,1)S(1)} collective-permute-done((bf16[4,13,16,128]{3,2,1,0:T(8,128)(2,1)S(1)}, bf16[4,13,16,128]{3,2,1,0:T(8,128)(2,1)S(1)}, u32[]{:S(2)}, u32[]{:S(2)}) %collective-permute-start.2) | collective-permute-done | bytes 213024 | tf_op jit(solution)/shard_map/ppermute | solution.py:142
  90.3 1.2 collective-permute-done.3
  91.5 1.9 %collective-permute-start.5 = (bf16[4,25,16,128]{3,2,1,0:T(8,128)(2,1)S(1)}, bf16[4,25,16,128]{3,2,1,0:T(8,128)(2,1)S(1)}, u32[]{:S(2)}, u32[]{:S(2)}) collective-permute-start(bf16[4,25,16,128]{3,2,1,0:T(8,128)(2,1)S(1)} %constant_dynamic-update-slice_fusion.refs_1_), channel_id=1, source_target_pairs={{0,64},{64,0},{1,65},{65,1},{2,66},{66,2},{3,67},{67,3},{4,68},{68... | collective-permute-start | bytes 1228808 | tf_op jit(solution)/shard_map/ppermute | solution.py:146
  93.5 1.7 %collective-permute-done.5.refs_3_ = bf16[4,25,16,128]{3,2,1,0:T(8,128)(2,1)S(1)} collective-permute-done((bf16[4,25,16,128]{3,2,1,0:T(8,128)(2,1)S(1)}, bf16[4,25,16,128]{3,2,1,0:T(8,128)(2,1)S(1)}, u32[]{:S(2)}, u32[]{:S(2)}) %collective-permute-start.5) | collective-permute-done | bytes 409632 | tf_op jit(solution)/shard_map/ppermute | solution.py:146
  95.2 0.0 collective-permute-done.4.refs_2_
  95.2 0.0 all-to-all-done.a_ref
  95.2 6.2 %product.1 = f32[16,400,128]{2,1,0:T(8,128)S(1)} custom-call(s32[1]{0:T(128)} %bitcast.place_ref, bf16[16,624,128]{2,1,0:T(8,128)(2,1)S(1)} %all-to-all-done.a_ref, bf16[3,4,25,16,128]{4,3,2,1,0:T(8,128)(2,1)} %pad_maximum_fusion.refs_0_, bf16[4,25,16,128]{3,2,1,0:T(8,128)(2,1)S(1)} %constant_dynamic-update-slice_fusion.refs_1_, ...), custom_call_target="tpu_custom_call" | custom-call | flops 2617245696 | bytes 11534336 | tf_op jit(solution)/shard_map/product/pallas_call | solution.py:82
  101.3 0.2 convert_element_type.6
  101.6 28.8 %all_to_all.20 = f16[16,400,128]{2,1,0:T(8,128)(2,1)S(1)} all-to-all(f16[16,400,128]{2,1,0:T(8,128)(2,1)S(1)} %convert_element_type.6), channel_id=1, replica_groups=mesh['y'=4,'core'=2,'zh'=4,'x'=4,'zl'=4] {'y','x'}, dimensions={0} | all-to-all | bytes 3276800 | tf_op jit(solution)/shard_map/all_to_all | solution.py:161
  130.4 0.2 convert_element_type.7
  130.6 0.2 fusion.3
  130.8 1.3 fusion.in_ref
  132.2 0.1 pack.1
  132.3 34.1 %all_to_all.21.in_ref = f32[16,32,128]{2,1,0:T(8,128)S(1)} all-to-all(f32[16,32,128]{2,1,0:T(8,128)S(1)} %pack.1), channel_id=1, replica_groups=mesh['y'=4,'core'=2,'zh'=4,'x'=4,'zl'=4] {'zh','zl'}, dimensions={0} | all-to-all | bytes 524288 | tf_op jit(solution)/shard_map/all_to_all | solution.py:166
  166.3 0.7 last_sum.1
  (5 shorter events, 0.1 us)
Async XLA Ops:
  1.8 15.2 %all-to-all-start.1 = ((bf16[4,25,16,128]{3,2,1,0:T(8,128)(2,1)}), bf16[4,25,16,128]{3,2,1,0:T(8,128)(2,1)S(1)}, u32[]{:S(2)}, u32[]{:S(2)}) async-start(bf16[4,25,16,128]{3,2,1,0:T(8,128)(2,1)} %bitcast.9), calls=%async_computation.1 | async-start | bytes 819200 | tf_op jit(solution)/shard_map/all_to_all | solution.py:153
  10.9 1.7 %copy-start = (bf16[48,25,1024]{2,0,1:T(8,128)(2,1)S(1)}, bf16[48,25,1024]{2,0,1:T(8,128)(2,1)}, u32[]{:S(2)}) copy-start(bf16[48,25,1024]{2,0,1:T(8,128)(2,1)} %param.2) | copy-start | bytes 7372804
  17.0 78.2 %all-to-all-start = ((bf16[16,624,128]{2,1,0:T(8,128)(2,1)}), bf16[16,624,128]{2,1,0:T(8,128)(2,1)S(1)}, u32[]{:S(2)}, u32[]{:S(2)}) async-start(bf16[16,624,128]{2,1,0:T(8,128)(2,1)} %reorder.1), calls=%async_computation | async-start | bytes 5111808 | tf_op jit(solution)/shard_map/all_to_all | solution.py:155
  21.9 44.8 %collective-permute-start.1 = (bf16[4,25,16,128]{3,2,1,0:T(8,128)(2,1)S(1)}, bf16[4,25,16,128]{3,2,1,0:T(8,128)(2,1)S(1)}, u32[]{:S(2)}, u32[]{:S(2)}) collective-permute-start(bf16[4,25,16,128]{3,2,1,0:T(8,128)(2,1)S(1)} %all-to-all-done.1), channel_id=1, source_target_pairs={{0,48},{16,0},{32,16},{48,32},{1,49},{17,1},{33,17},{49,33},{2,50}... | collective-permute-start | bytes 1228808 | tf_op jit(solution)/shard_map/ppermute | solution.py:142
  32.7 34.0 %collective-permute-start = (bf16[4,25,16,128]{3,2,1,0:T(8,128)(2,1)S(1)}, bf16[4,25,16,128]{3,2,1,0:T(8,128)(2,1)S(1)}, u32[]{:S(2)}, u32[]{:S(2)}) collective-permute-start(bf16[4,25,16,128]{3,2,1,0:T(8,128)(2,1)S(1)} %all-to-all-done.1), channel_id=1, source_target_pairs={{0,16},{16,32},{32,48},{48,0},{1,17},{17,33},{33,49},{49,1},{2,18}... | collective-permute-start | bytes 1228808 | tf_op jit(solution)/shard_map/ppermute | solution.py:142
  67.9 27.3 %collective-permute-start.4 = (bf16[3,4,25,16,128]{4,3,2,1,0:T(8,128)(2,1)}, bf16[3,4,25,16,128]{4,3,2,1,0:T(8,128)(2,1)}, u32[]{:S(2)}, u32[]{:S(2)}) collective-permute-start(bf16[3,4,25,16,128]{4,3,2,1,0:T(8,128)(2,1)} %pad_maximum_fusion.refs_0_), channel_id=1, source_target_pairs={{0,64},{64,0},{1,65},{65,1},{2,66},{66,2},{3,67},{67,3},{4,68},{68... | collective-permute-start | bytes 3686408 | tf_op jit(solution)/shard_map/ppermute | solution.py:146
  69.8 20.5 %collective-permute-start.2 = (bf16[4,13,16,128]{3,2,1,0:T(8,128)(2,1)S(1)}, bf16[4,13,16,128]{3,2,1,0:T(8,128)(2,1)S(1)}, u32[]{:S(2)}, u32[]{:S(2)}) collective-permute-start(bf16[4,13,16,128]{3,2,1,0:T(8,128)(2,1)S(1)} %slice.16), channel_id=1, source_target_pairs={{0,16},{16,32},{32,48},{48,0},{1,17},{17,33},{33,49},{49,1},{2,18}... | collective-permute-start | bytes 638984 | tf_op jit(solution)/shard_map/ppermute | solution.py:142
  76.0 15.5 %collective-permute-start.3 = (bf16[4,12,16,128]{3,2,1,0:T(8,128)(2,1)S(1)}, bf16[4,12,16,128]{3,2,1,0:T(8,128)(2,1)S(1)}, u32[]{:S(2)}, u32[]{:S(2)}) collective-permute-start(bf16[4,12,16,128]{3,2,1,0:T(8,128)(2,1)S(1)} %slice.17), channel_id=1, source_target_pairs={{0,48},{16,0},{32,16},{48,32},{1,49},{17,1},{33,17},{49,33},{2,50}... | collective-permute-start | bytes 589832 | tf_op jit(solution)/shard_map/ppermute | solution.py:142
  91.5 3.6 %collective-permute-start.5 = (bf16[4,25,16,128]{3,2,1,0:T(8,128)(2,1)S(1)}, bf16[4,25,16,128]{3,2,1,0:T(8,128)(2,1)S(1)}, u32[]{:S(2)}, u32[]{:S(2)}) collective-permute-start(bf16[4,25,16,128]{3,2,1,0:T(8,128)(2,1)S(1)} %constant_dynamic-update-slice_fusion.refs_1_), channel_id=1, source_target_pairs={{0,64},{64,0},{1,65},{65,1},{2,66},{66,2},{3,67},{67,3},{4,68},{68... | collective-permute-start | bytes 1228808 | tf_op jit(solution)/shard_map/ppermute | solution.py:146

commit v4 on v3

--- a/solution.py
+++ b/solution.py
@@ -95,16 +95,15 @@
     for zh in range(4):
         turned = in_ref[zh * 96:(zh + 1) * 96].T
         for zl in range(4):
-            at = zl * 16
-            out_ref[zh * 4 + zl, :16, :96] = turned[at:at + 16]
-            out_ref[zh * 4 + zl, 16:, :96] = turned[64 + at:64 + at + 16]
-            out_ref[zh * 4 + zl, :, 96:] = jnp.zeros((32, 32), F32)
+            low, high = turned[zl * 16:zl * 16 + 16], turned[64 + zl * 16:64 + zl * 16 + 16]
+            out_ref[zh * 4 + zl, :16] = jnp.concatenate([low, high[:, :32]], axis=1)
+            out_ref[zh * 4 + zl, 16:] = jnp.concatenate([high[:8, 32:], high[8:, 32:]], axis=1)
 
 
 def pack(total):
     return pl.pallas_call(
         pack_kernel,
-        out_shape=jax.ShapeDtypeStruct((16, 32, 128), F32),
+        out_shape=jax.ShapeDtypeStruct((16, 24, 128), F32),
         in_specs=[VMEM],
         out_specs=VMEM,
         compiler_params=params(),
@@ -116,8 +115,9 @@
 def last_sum_kernel(in_ref, out_ref):
     for zh in range(4):
         total = in_ref[4 * zh] + in_ref[4 * zh + 1] + in_ref[4 * zh + 2] + in_ref[4 * zh + 3]
-        for half in range(2):
-            out_ref[:, zh * 192 + half * 96:zh * 192 + half * 96 + 96] = total[half * 16:half * 16 + 16, :96]
+        out_ref[:, zh * 192:zh * 192 + 128] = total[:16]
+        out_ref[:8, zh * 192 + 128:zh * 192 + 192] = total[16:, :64]
+        out_ref[8:, zh * 192 + 128:zh * 192 + 192] = total[16:, 64:]
 
 
 def last_sum(parts):
@@ -154,9 +154,12 @@
     sent = reorder(amplitudes.transpose(1, 0, 2), source_of_lane(zh))
     rows = lax.all_to_all(sent, ("y", "x"), 0, 0, tiled=True)
 
-    below, above = shift(own, "zh", 1), shift(own, "zh", -1)
-    near = jnp.stack([own, below, above])
-    far = jnp.concatenate([shift(below[:, :13], "zh", 1), shift(above[:, 13:], "zh", -1)], axis=1)
+    first, second = own[:, :13], own[:, 13:]
+    below, above = shift(first, "zh", 1), shift(second, "zh", -1)
+    far = jnp.concatenate([shift(below, "zh", 1), shift(above, "zh", -1)], axis=1)
+    below = jnp.concatenate([below, shift(second, "zh", 1)], axis=1)
+    above = jnp.concatenate([shift(first, "zh", -1), above], axis=1)
+    near, far = lax.optimization_barrier((jnp.stack([own, below, above]), far))
     part = product(place, rows, near, far, swap(near), swap(far)).astype(jnp.float16)
     arrived = lax.all_to_all(part, ("y", "x"), 0, 0, tiled=True).astype(F32)
     scale = jnp.exp2(arrived[:, 384:385, :1] - 7.0)

time: 170 us -> 165 us (0.971)
  blocking collectives: 62.9 us -> 51.2 us
  starting transfers between devices: 40.6 us -> 50.4 us
  waiting for transfers between devices: 45.2 us -> 42 us
    all_to_all x1, blocking collectives: 34.1 us -> 22.1 us  [local(): final = lax.all_to_all(pack(total), ('zh', 'zl'), 0, 0, tiled=True)]
    ppermute x4 -> x6, starting transfers between devices: 22.9 us -> 32.2 us  [shift(): return lax.ppermute(value, axis, [(i, (i + by) % 4) for i in range(4)])]
    ppermute x4 -> x6, waiting for transfers between devices: 43.5 us -> 40.7 us  [shift(): return lax.ppermute(value, axis, [(i, (i + by) % 4) for i in range(4)])]
  transfers between devices with their start and end apart: 8 -> 10, of which waited for: 4 -> 4; matrix products, arithmetic and copies ran while one was open for 1% -> 1% of each run, Pallas kernels for 3% -> 3%
where the time goes in v4:
time: 165 us; the launch traced here: 162 us
  blocking collectives  51.2 us (31%)
  starting transfers between devices  50.4 us (31%)
  waiting for transfers between devices  42 us (25%)
  Pallas kernels  11.6 us (7%)
  local copies, waits for them, and re-layouts  3.52 us (2%)
  other arithmetic  3.34 us (2%)
    ppermute x6, waiting for transfers between devices, shift(): return lax.ppermute(value, axis, [(i, (i + by) % 4) for i in range(4)])  40.7 us
    ppermute x6, starting transfers between devices, shift(): return lax.ppermute(value, axis, [(i, (i + by) % 4) for i in range(4)])  32.2 us
    all_to_all x1, blocking collectives, local(): arrived = lax.all_to_all(part, ('y', 'x'), 0, 0, tiled=True).astype(F32)  29.1 us
    all_to_all x1, blocking collectives, local(): final = lax.all_to_all(pack(total), ('zh', 'zl'), 0, 0, tiled=True)  22.1 us
    all_to_all x1, starting transfers between devices, local(): own = lax.all_to_all(by_y, 'y', 0, 0, tiled=True)  9.03 us
    pallas_call x1, Pallas kernels, product(): pl.pallas_call(product_kernel, out_shape=jax.ShapeDtypeStruct((16, 400, 1...  6.17 us
    all_to_all x1, starting transfers between devices, local(): rows = lax.all_to_all(sent, ('y', 'x'), 0, 0, tiled=True)  4.85 us
    pallas_call x1, Pallas kernels, reorder(): pl.pallas_call(reorder_kernel, out_shape=jax.ShapeDtypeStruct((16, PAIRS...  4.46 us
  transfers between devices with their start and end apart: 10, of which 4 were waited for; matrix products, arithmetic and copies ran while one was open for 1% of the time, Pallas kernels for 3%

profile of v4, /device:TPU:24, one launch (start us, length us, event | category | flops | bytes accessed | tf_op | source)
XLA Modules:
  0.0 162.3 jit_solution(13826112032365082145)
XLA Ops:
  0.0 1.8 %copy.5 = bf16[25,4,16,128]{3,2,0,1:T(8,128)(2,1)} copy(bf16[25,4,16,128]{3,2,1,0:T(8,128)(2,1)} %bitcast.14) | data formatting | bytes 819200 | tf_op jit(solution)/shard_map/reshape | solution.py:152
  1.8 9.0 %all-to-all-start.1 = ((bf16[4,25,16,128]{3,2,1,0:T(8,128)(2,1)}), bf16[4,25,16,128]{3,2,1,0:T(8,128)(2,1)S(1)}, u32[]{:S(2)}, u32[]{:S(2)}) async-start(bf16[4,25,16,128]{3,2,1,0:T(8,128)(2,1)} %bitcast.11), calls=%async_computation.1 | async-start | bytes 819200 | tf_op jit(solution)/shard_map/all_to_all | solution.py:153
  10.9 0.0 copy-start
  10.9 1.7 %copy-done = bf16[48,25,1024]{2,0,1:T(8,128)(2,1)S(1)} copy-done((bf16[48,25,1024]{2,0,1:T(8,128)(2,1)S(1)}, bf16[48,25,1024]{2,0,1:T(8,128)(2,1)}, u32[]{:S(2)}) %copy-start) | copy-done | bytes 2457624
  12.6 4.5 %reorder.1 = bf16[16,624,128]{2,1,0:T(8,128)(2,1)} custom-call(bf16[25,48,1024]{2,1,0:T(8,128)(2,1)S(1)} %bitcast.12, s32[1,1024]{1,0:T(1,128)S(1)} %fusion.4.src_ref), custom_call_target="tpu_custom_call" | custom-call | flops 2617245696 | bytes 5242880 | tf_op jit(solution)/shard_map/reorder/pallas_call | solution.py:42
  17.0 0.0 all-to-all-done.1
  17.0 4.9 %all-to-all-start = ((bf16[16,624,128]{2,1,0:T(8,128)(2,1)}), bf16[16,624,128]{2,1,0:T(8,128)(2,1)S(1)}, u32[]{:S(2)}, u32[]{:S(2)}) async-start(bf16[16,624,128]{2,1,0:T(8,128)(2,1)} %reorder.1), calls=%async_computation | async-start | bytes 5111808 | tf_op jit(solution)/shard_map/all_to_all | solution.py:155
  21.9 7.2 %collective-permute-start = (bf16[4,13,16,128]{3,2,1,0:T(8,128)(2,1)S(1)}, bf16[4,13,16,128]{3,2,1,0:T(8,128)(2,1)S(1)}, u32[]{:S(2)}, u32[]{:S(2)}) collective-permute-start(bf16[4,13,16,128]{3,2,1,0:T(8,128)(2,1)S(1)} %slice.16), channel_id=1, source_target_pairs={{0,16},{16,32},{32,48},{48,0},{1,17},{17,33},{33,49},{49,1},{2,18}... | collective-permute-start | bytes 638984 | tf_op jit(solution)/shard_map/ppermute | solution.py:142
  29.1 5.6 %collective-permute-start.2 = (bf16[4,13,16,128]{3,2,1,0:T(8,128)(2,1)S(1)}, bf16[4,13,16,128]{3,2,1,0:T(8,128)(2,1)S(1)}, u32[]{:S(2)}, u32[]{:S(2)}) collective-permute-start(bf16[4,13,16,128]{3,2,1,0:T(8,128)(2,1)S(1)} %slice.16), channel_id=1, source_target_pairs={{0,48},{16,0},{32,16},{48,32},{1,49},{17,1},{33,17},{49,33},{2,50}... | collective-permute-start | bytes 638984 | tf_op jit(solution)/shard_map/ppermute | solution.py:142
  34.7 7.8 %collective-permute-start.3 = (bf16[4,12,16,128]{3,2,1,0:T(8,128)(2,1)S(1)}, bf16[4,12,16,128]{3,2,1,0:T(8,128)(2,1)S(1)}, u32[]{:S(2)}, u32[]{:S(2)}) collective-permute-start(bf16[4,12,16,128]{3,2,1,0:T(8,128)(2,1)S(1)} %slice.17), channel_id=1, source_target_pairs={{0,48},{16,0},{32,16},{48,32},{1,49},{17,1},{33,17},{49,33},{2,50}... | collective-permute-start | bytes 589832 | tf_op jit(solution)/shard_map/ppermute | solution.py:142
  42.5 1.9 %collective-permute-start.1 = (bf16[4,12,16,128]{3,2,1,0:T(8,128)(2,1)S(1)}, bf16[4,12,16,128]{3,2,1,0:T(8,128)(2,1)S(1)}, u32[]{:S(2)}, u32[]{:S(2)}) collective-permute-start(bf16[4,12,16,128]{3,2,1,0:T(8,128)(2,1)S(1)} %slice.17), channel_id=1, source_target_pairs={{0,16},{16,32},{32,48},{48,0},{1,17},{17,33},{33,49},{49,1},{2,18}... | collective-permute-start | bytes 589832 | tf_op jit(solution)/shard_map/ppermute | solution.py:142
  44.4 28.7 %collective-permute-done.3 = bf16[4,12,16,128]{3,2,1,0:T(8,128)(2,1)S(1)} collective-permute-done((bf16[4,12,16,128]{3,2,1,0:T(8,128)(2,1)S(1)}, bf16[4,12,16,128]{3,2,1,0:T(8,128)(2,1)S(1)}, u32[]{:S(2)}, u32[]{:S(2)}) %collective-permute-start.3) | collective-permute-done | bytes 196640 | tf_op jit(solution)/shard_map/ppermute | solution.py:142
  73.2 4.2 %collective-permute-start.5 = (bf16[4,12,16,128]{3,2,1,0:T(8,128)(2,1)S(1)}, bf16[4,12,16,128]{3,2,1,0:T(8,128)(2,1)S(1)}, u32[]{:S(2)}, u32[]{:S(2)}) collective-permute-start(bf16[4,12,16,128]{3,2,1,0:T(8,128)(2,1)S(1)} %collective-permute-done.3), channel_id=1, source_target_pairs={{0,48},{16,0},{32,16},{48,32},{1,49},{17,1},{33,17},{49,33},{2,50}... | collective-permute-start | bytes 589832 | tf_op jit(solution)/shard_map/ppermute | solution.py:142
  77.4 0.0 collective-permute-done
  77.5 5.5 %collective-permute-start.4 = (bf16[4,13,16,128]{3,2,1,0:T(8,128)(2,1)S(1)}, bf16[4,13,16,128]{3,2,1,0:T(8,128)(2,1)S(1)}, u32[]{:S(2)}, u32[]{:S(2)}) collective-permute-start(bf16[4,13,16,128]{3,2,1,0:T(8,128)(2,1)S(1)} %collective-permute-done), channel_id=1, source_target_pairs={{0,16},{16,32},{32,48},{48,0},{1,17},{17,33},{33,49},{49,1},{2,18}... | collective-permute-start | bytes 638984 | tf_op jit(solution)/shard_map/ppermute | solution.py:142
  83.0 0.0 collective-permute-done.2
  83.0 0.0 collective-permute-done.1
  83.1 1.2 pad_maximum_fusion.refs_0_
  84.3 9.1 %collective-permute-done.5 = bf16[4,12,16,128]{3,2,1,0:T(8,128)(2,1)S(1)} collective-permute-done((bf16[4,12,16,128]{3,2,1,0:T(8,128)(2,1)S(1)}, bf16[4,12,16,128]{3,2,1,0:T(8,128)(2,1)S(1)}, u32[]{:S(2)}, u32[]{:S(2)}) %collective-permute-start.5) | collective-permute-done | bytes 196640 | tf_op jit(solution)/shard_map/ppermute | solution.py:142
  93.4 2.8 %collective-permute-done.4 = bf16[4,13,16,128]{3,2,1,0:T(8,128)(2,1)S(1)} collective-permute-done((bf16[4,13,16,128]{3,2,1,0:T(8,128)(2,1)S(1)}, bf16[4,13,16,128]{3,2,1,0:T(8,128)(2,1)S(1)}, u32[]{:S(2)}, u32[]{:S(2)}) %collective-permute-start.4) | collective-permute-done | bytes 213024 | tf_op jit(solution)/shard_map/ppermute | solution.py:142
  96.2 1.9 %collective-permute-start.6 = (bf16[3,4,25,16,128]{4,3,2,1,0:T(8,128)(2,1)}, bf16[3,4,25,16,128]{4,3,2,1,0:T(8,128)(2,1)}, u32[]{:S(2)}, u32[]{:S(2)}) collective-permute-start(bf16[3,4,25,16,128]{4,3,2,1,0:T(8,128)(2,1)} %pad_maximum_fusion.refs_0_), channel_id=1, source_target_pairs={{0,64},{64,0},{1,65},{65,1},{2,66},{66,2},{3,67},{67,3},{4,68},{68... | collective-permute-start | bytes 3686408 | tf_op jit(solution)/shard_map/ppermute | solution.py:146
  98.1 2.4 %collective-permute-start.7 = (bf16[4,25,16,128]{3,2,1,0:T(8,128)(2,1)S(1)}, bf16[4,25,16,128]{3,2,1,0:T(8,128)(2,1)S(1)}, u32[]{:S(2)}, u32[]{:S(2)}) collective-permute-start(bf16[4,25,16,128]{3,2,1,0:T(8,128)(2,1)S(1)} %pad_maximum_fusion.1.refs_1_), channel_id=1, source_target_pairs={{0,64},{64,0},{1,65},{65,1},{2,66},{66,2},{3,67},{67,3},{4,68},{68... | collective-permute-start | bytes 1228808 | tf_op jit(solution)/shard_map/ppermute | solution.py:146
  100.6 1.3 collective-permute-done.7.refs_3_
  101.9 0.0 collective-permute-done.6.refs_2_
  101.9 0.0 all-to-all-done.a_ref
  101.9 6.2 %product.1 = f32[16,400,128]{2,1,0:T(8,128)S(1)} custom-call(s32[1]{0:T(128)} %bitcast.place_ref, bf16[16,624,128]{2,1,0:T(8,128)(2,1)S(1)} %all-to-all-done.a_ref, bf16[3,4,25,16,128]{4,3,2,1,0:T(8,128)(2,1)} %pad_maximum_fusion.refs_0_, bf16[4,25,16,128]{3,2,1,0:T(8,128)(2,1)S(1)} %pad_maximum_fusion.1.refs_1_, ...), custom_call_target="tpu_custom_call" | custom-call | flops 2617245696 | bytes 11534336 | tf_op jit(solution)/shard_map/product/pallas_call | solution.py:82
  108.1 0.2 convert_element_type.6
  108.3 29.1 %all_to_all.20 = f16[16,400,128]{2,1,0:T(8,128)(2,1)S(1)} all-to-all(f16[16,400,128]{2,1,0:T(8,128)(2,1)S(1)} %convert_element_type.6), channel_id=1, replica_groups=mesh['y'=4,'core'=2,'zh'=4,'x'=4,'zl'=4] {'y','x'}, dimensions={0} | all-to-all | bytes 3276800 | tf_op jit(solution)/shard_map/all_to_all | solution.py:164
  137.4 0.2 convert_element_type.7
  137.7 0.2 fusion.3
  137.9 1.3 fusion.in_ref
  139.2 0.3 pack.1
  139.5 22.1 %all_to_all.21.in_ref = f32[16,24,128]{2,1,0:T(8,128)S(1)} all-to-all(f32[16,24,128]{2,1,0:T(8,128)S(1)} %pack.1), channel_id=1, replica_groups=mesh['y'=4,'core'=2,'zh'=4,'x'=4,'zl'=4] {'zh','zl'}, dimensions={0} | all-to-all | bytes 393216 | tf_op jit(solution)/shard_map/all_to_all | solution.py:169
  161.6 0.7 last_sum.1
  (6 shorter events, 0.2 us)
Async XLA Ops:
  1.8 15.2 %all-to-all-start.1 = ((bf16[4,25,16,128]{3,2,1,0:T(8,128)(2,1)}), bf16[4,25,16,128]{3,2,1,0:T(8,128)(2,1)S(1)}, u32[]{:S(2)}, u32[]{:S(2)}) async-start(bf16[4,25,16,128]{3,2,1,0:T(8,128)(2,1)} %bitcast.11), calls=%async_computation.1 | async-start | bytes 819200 | tf_op jit(solution)/shard_map/all_to_all | solution.py:153
  10.9 1.7 %copy-start = (bf16[48,25,1024]{2,0,1:T(8,128)(2,1)S(1)}, bf16[48,25,1024]{2,0,1:T(8,128)(2,1)}, u32[]{:S(2)}) copy-start(bf16[48,25,1024]{2,0,1:T(8,128)(2,1)} %param.2) | copy-start | bytes 7372804
  17.0 84.9 %all-to-all-start = ((bf16[16,624,128]{2,1,0:T(8,128)(2,1)}), bf16[16,624,128]{2,1,0:T(8,128)(2,1)S(1)}, u32[]{:S(2)}, u32[]{:S(2)}) async-start(bf16[16,624,128]{2,1,0:T(8,128)(2,1)} %reorder.1), calls=%async_computation | async-start | bytes 5111808 | tf_op jit(solution)/shard_map/all_to_all | solution.py:155
  21.9 55.5 %collective-permute-start = (bf16[4,13,16,128]{3,2,1,0:T(8,128)(2,1)S(1)}, bf16[4,13,16,128]{3,2,1,0:T(8,128)(2,1)S(1)}, u32[]{:S(2)}, u32[]{:S(2)}) collective-permute-start(bf16[4,13,16,128]{3,2,1,0:T(8,128)(2,1)S(1)} %slice.16), channel_id=1, source_target_pairs={{0,16},{16,32},{32,48},{48,0},{1,17},{17,33},{33,49},{49,1},{2,18}... | collective-permute-start | bytes 638984 | tf_op jit(solution)/shard_map/ppermute | solution.py:142
  29.1 53.9 %collective-permute-start.2 = (bf16[4,13,16,128]{3,2,1,0:T(8,128)(2,1)S(1)}, bf16[4,13,16,128]{3,2,1,0:T(8,128)(2,1)S(1)}, u32[]{:S(2)}, u32[]{:S(2)}) collective-permute-start(bf16[4,13,16,128]{3,2,1,0:T(8,128)(2,1)S(1)} %slice.16), channel_id=1, source_target_pairs={{0,48},{16,0},{32,16},{48,32},{1,49},{17,1},{33,17},{49,33},{2,50}... | collective-permute-start | bytes 638984 | tf_op jit(solution)/shard_map/ppermute | solution.py:142
  34.7 38.5 %collective-permute-start.3 = (bf16[4,12,16,128]{3,2,1,0:T(8,128)(2,1)S(1)}, bf16[4,12,16,128]{3,2,1,0:T(8,128)(2,1)S(1)}, u32[]{:S(2)}, u32[]{:S(2)}) collective-permute-start(bf16[4,12,16,128]{3,2,1,0:T(8,128)(2,1)S(1)} %slice.17), channel_id=1, source_target_pairs={{0,48},{16,0},{32,16},{48,32},{1,49},{17,1},{33,17},{49,33},{2,50}... | collective-permute-start | bytes 589832 | tf_op jit(solution)/shard_map/ppermute | solution.py:142
  42.5 40.5 %collective-permute-start.1 = (bf16[4,12,16,128]{3,2,1,0:T(8,128)(2,1)S(1)}, bf16[4,12,16,128]{3,2,1,0:T(8,128)(2,1)S(1)}, u32[]{:S(2)}, u32[]{:S(2)}) collective-permute-start(bf16[4,12,16,128]{3,2,1,0:T(8,128)(2,1)S(1)} %slice.17), channel_id=1, source_target_pairs={{0,16},{16,32},{32,48},{48,0},{1,17},{17,33},{33,49},{49,1},{2,18}... | collective-permute-start | bytes 589832 | tf_op jit(solution)/shard_map/ppermute | solution.py:142
  73.2 20.2 %collective-permute-start.5 = (bf16[4,12,16,128]{3,2,1,0:T(8,128)(2,1)S(1)}, bf16[4,12,16,128]{3,2,1,0:T(8,128)(2,1)S(1)}, u32[]{:S(2)}, u32[]{:S(2)}) collective-permute-start(bf16[4,12,16,128]{3,2,1,0:T(8,128)(2,1)S(1)} %collective-permute-done.3), channel_id=1, source_target_pairs={{0,48},{16,0},{32,16},{48,32},{1,49},{17,1},{33,17},{49,33},{2,50}... | collective-permute-start | bytes 589832 | tf_op jit(solution)/shard_map/ppermute | solution.py:142
  77.5 18.7 %collective-permute-start.4 = (bf16[4,13,16,128]{3,2,1,0:T(8,128)(2,1)S(1)}, bf16[4,13,16,128]{3,2,1,0:T(8,128)(2,1)S(1)}, u32[]{:S(2)}, u32[]{:S(2)}) collective-permute-start(bf16[4,13,16,128]{3,2,1,0:T(8,128)(2,1)S(1)} %collective-permute-done), channel_id=1, source_target_pairs={{0,16},{16,32},{32,48},{48,0},{1,17},{17,33},{33,49},{49,1},{2,18}... | collective-permute-start | bytes 638984 | tf_op jit(solution)/shard_map/ppermute | solution.py:142
  96.2 5.7 %collective-permute-start.6 = (bf16[3,4,25,16,128]{4,3,2,1,0:T(8,128)(2,1)}, bf16[3,4,25,16,128]{4,3,2,1,0:T(8,128)(2,1)}, u32[]{:S(2)}, u32[]{:S(2)}) collective-permute-start(bf16[3,4,25,16,128]{4,3,2,1,0:T(8,128)(2,1)} %pad_maximum_fusion.refs_0_), channel_id=1, source_target_pairs={{0,64},{64,0},{1,65},{65,1},{2,66},{66,2},{3,67},{67,3},{4,68},{68... | collective-permute-start | bytes 3686408 | tf_op jit(solution)/shard_map/ppermute | solution.py:146
  98.1 3.8 %collective-permute-start.7 = (bf16[4,25,16,128]{3,2,1,0:T(8,128)(2,1)S(1)}, bf16[4,25,16,128]{3,2,1,0:T(8,128)(2,1)S(1)}, u32[]{:S(2)}, u32[]{:S(2)}) collective-permute-start(bf16[4,25,16,128]{3,2,1,0:T(8,128)(2,1)S(1)} %pad_maximum_fusion.1.refs_1_), channel_id=1, source_target_pairs={{0,64},{64,0},{1,65},{65,1},{2,66},{66,2},{3,67},{67,3},{4,68},{68... | collective-permute-start | bytes 1228808 | tf_op jit(solution)/shard_map/ppermute | solution.py:146

commit v5 on v4

--- a/solution.py
+++ b/solution.py
@@ -67,21 +67,16 @@
             [a_ref[4 * y:4 * y + 4, p * ROWS:(p + 1) * ROWS, :].reshape(192, 128) for p in range(PAIRS)], axis=1
         )
         block = jnp.dot(left, right_ref[...], preferred_element_type=F32)
-        largest = jnp.max(jnp.max(jnp.abs(block), axis=0, keepdims=True), axis=1, keepdims=True)
-        exponent = jnp.ceil(jnp.log2(jnp.maximum(largest, 2.0 ** -100)))
-        block = block * jnp.exp2(7.0 - exponent)
-        block = block * jnp.abs(block)
         for x in range(4):
             for j in range(4):
                 part = block[:, j * 256 + x * 64:j * 256 + (x + 1) * 64]
                 out_ref[y * 4 + x, j * 96:(j + 1) * 96] = jnp.concatenate([part[:96], part[96:]], axis=1)
-            out_ref[y * 4 + x, 384:] = jnp.broadcast_to(exponent, (16, 128))
 
 
 def product(place, a, near, far, near_other, far_other):
     return pl.pallas_call(
         product_kernel,
-        out_shape=jax.ShapeDtypeStruct((16, 400, 128), F32),
+        out_shape=jax.ShapeDtypeStruct((16, 384, 128), F32),
         in_specs=[SMEM] + [VMEM] * 5,
         out_specs=VMEM,
         scratch_shapes=[pltpu.VMEM((DEPTH, 1024), BF16)],
@@ -160,12 +155,9 @@
     below = jnp.concatenate([below, shift(second, "zh", 1)], axis=1)
     above = jnp.concatenate([shift(first, "zh", -1), above], axis=1)
     near, far = lax.optimization_barrier((jnp.stack([own, below, above]), far))
-    part = product(place, rows, near, far, swap(near), swap(far)).astype(jnp.float16)
-    arrived = lax.all_to_all(part, ("y", "x"), 0, 0, tiled=True).astype(F32)
-    scale = jnp.exp2(arrived[:, 384:385, :1] - 7.0)
-    coded = arrived[:, :384]
-    root = jnp.sqrt(jnp.abs(coded)) * scale
-    total = jnp.sum(jnp.where(coded < 0, -root, root), axis=0)
+    part = product(place, rows, near, far, swap(near), swap(far))
+    arrived = lax.all_to_all(part, ("y", "x"), 0, 0, tiled=True)
+    total = jnp.sum(arrived, axis=0)
     final = lax.all_to_all(pack(total), ("zh", "zl"), 0, 0, tiled=True)
     return last_sum(final).T
 

time: 165 us -> 179 us (1.085)
  blocking collectives: 51.2 us -> 67.3 us
  other arithmetic: 3.34 us -> 1.49 us
    all_to_all x1, blocking collectives: 29.1 us -> 45.1 us  [local(): arrived = lax.all_to_all(part, ('y', 'x'), 0, 0, tiled=True)]
where the time goes in v5:
time: 179 us; the launch traced here: 176 us
  blocking collectives  67.3 us (38%)
  starting transfers between devices  50.4 us (28%)
  waiting for transfers between devices  42 us (23%)
  Pallas kernels  11.2 us (6%)
  local copies, waits for them, and re-layouts  3.51 us (2%)
    all_to_all x1, blocking collectives, local(): arrived = lax.all_to_all(part, ('y', 'x'), 0, 0, tiled=True)  45.1 us
    ppermute x6, waiting for transfers between devices, shift(): return lax.ppermute(value, axis, [(i, (i + by) % 4) for i in range(4)])  40.6 us
    ppermute x6, starting transfers between devices, shift(): return lax.ppermute(value, axis, [(i, (i + by) % 4) for i in range(4)])  32.2 us
    all_to_all x1, blocking collectives, local(): final = lax.all_to_all(pack(total), ('zh', 'zl'), 0, 0, tiled=True)  22.2 us
    all_to_all x1, starting transfers between devices, local(): own = lax.all_to_all(by_y, 'y', 0, 0, tiled=True)  9.03 us
    pallas_call x1, Pallas kernels, product(): pl.pallas_call(product_kernel, out_shape=jax.ShapeDtypeStruct((16, 384, 1...  5.73 us
    all_to_all x1, starting transfers between devices, local(): rows = lax.all_to_all(sent, ('y', 'x'), 0, 0, tiled=True)  4.83 us
    pallas_call x1, Pallas kernels, reorder(): pl.pallas_call(reorder_kernel, out_shape=jax.ShapeDtypeStruct((16, PAIRS...  4.48 us
  transfers between devices with their start and end apart: 10, of which 4 were waited for; matrix products, arithmetic and copies ran while one was open for 1% of the time, Pallas kernels for 3%

profile of v5, /device:TPU:24, one launch (start us, length us, event | category | flops | bytes accessed | tf_op | source)
XLA Modules:
  0.0 176.0 jit_solution(5379503419276810746)
XLA Ops:
  0.0 1.8 %copy.5 = bf16[25,4,16,128]{3,2,0,1:T(8,128)(2,1)} copy(bf16[25,4,16,128]{3,2,1,0:T(8,128)(2,1)} %bitcast.14) | data formatting | bytes 819200 | tf_op jit(solution)/shard_map/reshape | solution.py:147
  1.8 9.0 %all-to-all-start.1 = ((bf16[4,25,16,128]{3,2,1,0:T(8,128)(2,1)}), bf16[4,25,16,128]{3,2,1,0:T(8,128)(2,1)S(1)}, u32[]{:S(2)}, u32[]{:S(2)}) async-start(bf16[4,25,16,128]{3,2,1,0:T(8,128)(2,1)} %bitcast.11), calls=%async_computation.1 | async-start | bytes 819200 | tf_op jit(solution)/shard_map/all_to_all | solution.py:148
  10.9 0.0 copy-start
  10.9 1.7 copy-done
  12.6 4.5 %reorder.1 = bf16[16,624,128]{2,1,0:T(8,128)(2,1)} custom-call(bf16[25,48,1024]{2,1,0:T(8,128)(2,1)S(1)} %bitcast.12, s32[1,1024]{1,0:T(1,128)S(1)} %fusion.src_ref), custom_call_target="tpu_custom_call" | custom-call | flops 2617245696 | bytes 5242880 | tf_op jit(solution)/shard_map/reorder/pallas_call | solution.py:42
  17.0 0.0 all-to-all-done.1
  17.0 4.8 %all-to-all-start = ((bf16[16,624,128]{2,1,0:T(8,128)(2,1)}), bf16[16,624,128]{2,1,0:T(8,128)(2,1)S(1)}, u32[]{:S(2)}, u32[]{:S(2)}) async-start(bf16[16,624,128]{2,1,0:T(8,128)(2,1)} %reorder.1), calls=%async_computation | async-start | bytes 5111808 | tf_op jit(solution)/shard_map/all_to_all | solution.py:150
  21.9 7.2 %collective-permute-start = (bf16[4,13,16,128]{3,2,1,0:T(8,128)(2,1)S(1)}, bf16[4,13,16,128]{3,2,1,0:T(8,128)(2,1)S(1)}, u32[]{:S(2)}, u32[]{:S(2)}) collective-permute-start(bf16[4,13,16,128]{3,2,1,0:T(8,128)(2,1)S(1)} %slice.8), channel_id=1, source_target_pairs={{0,16},{16,32},{32,48},{48,0},{1,17},{17,33},{33,49},{49,1},{2,18}... | collective-permute-start | bytes 638984 | tf_op jit(solution)/shard_map/ppermute | solution.py:137
  29.1 5.6 %collective-permute-start.2 = (bf16[4,13,16,128]{3,2,1,0:T(8,128)(2,1)S(1)}, bf16[4,13,16,128]{3,2,1,0:T(8,128)(2,1)S(1)}, u32[]{:S(2)}, u32[]{:S(2)}) collective-permute-start(bf16[4,13,16,128]{3,2,1,0:T(8,128)(2,1)S(1)} %slice.8), channel_id=1, source_target_pairs={{0,48},{16,0},{32,16},{48,32},{1,49},{17,1},{33,17},{49,33},{2,50}... | collective-permute-start | bytes 638984 | tf_op jit(solution)/shard_map/ppermute | solution.py:137
  34.7 7.8 %collective-permute-start.3 = (bf16[4,12,16,128]{3,2,1,0:T(8,128)(2,1)S(1)}, bf16[4,12,16,128]{3,2,1,0:T(8,128)(2,1)S(1)}, u32[]{:S(2)}, u32[]{:S(2)}) collective-permute-start(bf16[4,12,16,128]{3,2,1,0:T(8,128)(2,1)S(1)} %slice.9), channel_id=1, source_target_pairs={{0,48},{16,0},{32,16},{48,32},{1,49},{17,1},{33,17},{49,33},{2,50}... | collective-permute-start | bytes 589832 | tf_op jit(solution)/shard_map/ppermute | solution.py:137
  42.5 1.9 %collective-permute-start.1 = (bf16[4,12,16,128]{3,2,1,0:T(8,128)(2,1)S(1)}, bf16[4,12,16,128]{3,2,1,0:T(8,128)(2,1)S(1)}, u32[]{:S(2)}, u32[]{:S(2)}) collective-permute-start(bf16[4,12,16,128]{3,2,1,0:T(8,128)(2,1)S(1)} %slice.9), channel_id=1, source_target_pairs={{0,16},{16,32},{32,48},{48,0},{1,17},{17,33},{33,49},{49,1},{2,18}... | collective-permute-start | bytes 589832 | tf_op jit(solution)/shard_map/ppermute | solution.py:137
  44.5 28.7 %collective-permute-done.3 = bf16[4,12,16,128]{3,2,1,0:T(8,128)(2,1)S(1)} collective-permute-done((bf16[4,12,16,128]{3,2,1,0:T(8,128)(2,1)S(1)}, bf16[4,12,16,128]{3,2,1,0:T(8,128)(2,1)S(1)}, u32[]{:S(2)}, u32[]{:S(2)}) %collective-permute-start.3) | collective-permute-done | bytes 196640 | tf_op jit(solution)/shard_map/ppermute | solution.py:137
  73.2 4.2 %collective-permute-start.5 = (bf16[4,12,16,128]{3,2,1,0:T(8,128)(2,1)S(1)}, bf16[4,12,16,128]{3,2,1,0:T(8,128)(2,1)S(1)}, u32[]{:S(2)}, u32[]{:S(2)}) collective-permute-start(bf16[4,12,16,128]{3,2,1,0:T(8,128)(2,1)S(1)} %collective-permute-done.3), channel_id=1, source_target_pairs={{0,48},{16,0},{32,16},{48,32},{1,49},{17,1},{33,17},{49,33},{2,50}... | collective-permute-start | bytes 589832 | tf_op jit(solution)/shard_map/ppermute | solution.py:137
  77.4 0.0 collective-permute-done
  77.4 5.5 %collective-permute-start.4 = (bf16[4,13,16,128]{3,2,1,0:T(8,128)(2,1)S(1)}, bf16[4,13,16,128]{3,2,1,0:T(8,128)(2,1)S(1)}, u32[]{:S(2)}, u32[]{:S(2)}) collective-permute-start(bf16[4,13,16,128]{3,2,1,0:T(8,128)(2,1)S(1)} %collective-permute-done), channel_id=1, source_target_pairs={{0,16},{16,32},{32,48},{48,0},{1,17},{17,33},{33,49},{49,1},{2,18}... | collective-permute-start | bytes 638984 | tf_op jit(solution)/shard_map/ppermute | solution.py:137
  82.9 0.0 collective-permute-done.2
  83.0 0.0 collective-permute-done.1
  83.1 1.2 pad_maximum_fusion.refs_0_
  84.2 9.2 %collective-permute-done.5 = bf16[4,12,16,128]{3,2,1,0:T(8,128)(2,1)S(1)} collective-permute-done((bf16[4,12,16,128]{3,2,1,0:T(8,128)(2,1)S(1)}, bf16[4,12,16,128]{3,2,1,0:T(8,128)(2,1)S(1)}, u32[]{:S(2)}, u32[]{:S(2)}) %collective-permute-start.5) | collective-permute-done | bytes 196640 | tf_op jit(solution)/shard_map/ppermute | solution.py:137
  93.4 2.7 %collective-permute-done.4 = bf16[4,13,16,128]{3,2,1,0:T(8,128)(2,1)S(1)} collective-permute-done((bf16[4,13,16,128]{3,2,1,0:T(8,128)(2,1)S(1)}, bf16[4,13,16,128]{3,2,1,0:T(8,128)(2,1)S(1)}, u32[]{:S(2)}, u32[]{:S(2)}) %collective-permute-start.4) | collective-permute-done | bytes 213024 | tf_op jit(solution)/shard_map/ppermute | solution.py:137
  96.2 1.9 %collective-permute-start.6 = (bf16[3,4,25,16,128]{4,3,2,1,0:T(8,128)(2,1)}, bf16[3,4,25,16,128]{4,3,2,1,0:T(8,128)(2,1)}, u32[]{:S(2)}, u32[]{:S(2)}) collective-permute-start(bf16[3,4,25,16,128]{4,3,2,1,0:T(8,128)(2,1)} %pad_maximum_fusion.refs_0_), channel_id=1, source_target_pairs={{0,64},{64,0},{1,65},{65,1},{2,66},{66,2},{3,67},{67,3},{4,68},{68... | collective-permute-start | bytes 3686408 | tf_op jit(solution)/shard_map/ppermute | solution.py:141
  98.1 2.4 %collective-permute-start.7 = (bf16[4,25,16,128]{3,2,1,0:T(8,128)(2,1)S(1)}, bf16[4,25,16,128]{3,2,1,0:T(8,128)(2,1)S(1)}, u32[]{:S(2)}, u32[]{:S(2)}) collective-permute-start(bf16[4,25,16,128]{3,2,1,0:T(8,128)(2,1)S(1)} %pad_maximum_fusion.1.refs_1_), channel_id=1, source_target_pairs={{0,64},{64,0},{1,65},{65,1},{2,66},{66,2},{3,67},{67,3},{4,68},{68... | collective-permute-start | bytes 1228808 | tf_op jit(solution)/shard_map/ppermute | solution.py:141
  100.5 1.3 collective-permute-done.7.refs_3_
  101.9 0.0 collective-permute-done.6.refs_2_
  101.9 0.0 all-to-all-done.a_ref
  101.9 5.7 %product.1 = f32[16,384,128]{2,1,0:T(8,128)S(1)} custom-call(s32[1]{0:T(128)} %bitcast.place_ref, bf16[16,624,128]{2,1,0:T(8,128)(2,1)S(1)} %all-to-all-done.a_ref, bf16[3,4,25,16,128]{4,3,2,1,0:T(8,128)(2,1)} %pad_maximum_fusion.refs_0_, bf16[4,25,16,128]{3,2,1,0:T(8,128)(2,1)S(1)} %pad_maximum_fusion.1.refs_1_, ...), custom_call_target="tpu_custom_call" | custom-call | flops 2617245696 | bytes 11534336 | tf_op jit(solution)/shard_map/product/pallas_call | solution.py:77
  107.6 45.1 %all_to_all.20 = f32[16,384,128]{2,1,0:T(8,128)S(1)} all-to-all(f32[16,384,128]{2,1,0:T(8,128)S(1)} %product.1), channel_id=1, replica_groups=mesh['y'=4,'core'=2,'zh'=4,'x'=4,'zl'=4] {'y','x'}, dimensions={0} | all-to-all | bytes 6291456 | tf_op jit(solution)/shard_map/all_to_all | solution.py:159
  152.7 0.2 reduce_sum.9.in_ref
  152.9 0.3 pack.1
  153.2 22.2 %all_to_all.21.in_ref = f32[16,24,128]{2,1,0:T(8,128)S(1)} all-to-all(f32[16,24,128]{2,1,0:T(8,128)S(1)} %pack.1), channel_id=1, replica_groups=mesh['y'=4,'core'=2,'zh'=4,'x'=4,'zl'=4] {'zh','zl'}, dimensions={0} | all-to-all | bytes 393216 | tf_op jit(solution)/shard_map/all_to_all | solution.py:161
  175.3 0.7 last_sum.1
  (6 shorter events, 0.2 us)
Async XLA Ops:
  1.8 15.3 %all-to-all-start.1 = ((bf16[4,25,16,128]{3,2,1,0:T(8,128)(2,1)}), bf16[4,25,16,128]{3,2,1,0:T(8,128)(2,1)S(1)}, u32[]{:S(2)}, u32[]{:S(2)}) async-start(bf16[4,25,16,128]{3,2,1,0:T(8,128)(2,1)} %bitcast.11), calls=%async_computation.1 | async-start | bytes 819200 | tf_op jit(solution)/shard_map/all_to_all | solution.py:148
  10.9 1.7 copy-start
  17.0 84.8 %all-to-all-start = ((bf16[16,624,128]{2,1,0:T(8,128)(2,1)}), bf16[16,624,128]{2,1,0:T(8,128)(2,1)S(1)}, u32[]{:S(2)}, u32[]{:S(2)}) async-start(bf16[16,624,128]{2,1,0:T(8,128)(2,1)} %reorder.1), calls=%async_computation | async-start | bytes 5111808 | tf_op jit(solution)/shard_map/all_to_all | solution.py:150
  21.9 55.5 %collective-permute-start = (bf16[4,13,16,128]{3,2,1,0:T(8,128)(2,1)S(1)}, bf16[4,13,16,128]{3,2,1,0:T(8,128)(2,1)S(1)}, u32[]{:S(2)}, u32[]{:S(2)}) collective-permute-start(bf16[4,13,16,128]{3,2,1,0:T(8,128)(2,1)S(1)} %slice.8), channel_id=1, source_target_pairs={{0,16},{16,32},{32,48},{48,0},{1,17},{17,33},{33,49},{49,1},{2,18}... | collective-permute-start | bytes 638984 | tf_op jit(solution)/shard_map/ppermute | solution.py:137
  29.1 53.8 %collective-permute-start.2 = (bf16[4,13,16,128]{3,2,1,0:T(8,128)(2,1)S(1)}, bf16[4,13,16,128]{3,2,1,0:T(8,128)(2,1)S(1)}, u32[]{:S(2)}, u32[]{:S(2)}) collective-permute-start(bf16[4,13,16,128]{3,2,1,0:T(8,128)(2,1)S(1)} %slice.8), channel_id=1, source_target_pairs={{0,48},{16,0},{32,16},{48,32},{1,49},{17,1},{33,17},{49,33},{2,50}... | collective-permute-start | bytes 638984 | tf_op jit(solution)/shard_map/ppermute | solution.py:137
  34.7 38.5 %collective-permute-start.3 = (bf16[4,12,16,128]{3,2,1,0:T(8,128)(2,1)S(1)}, bf16[4,12,16,128]{3,2,1,0:T(8,128)(2,1)S(1)}, u32[]{:S(2)}, u32[]{:S(2)}) collective-permute-start(bf16[4,12,16,128]{3,2,1,0:T(8,128)(2,1)S(1)} %slice.9), channel_id=1, source_target_pairs={{0,48},{16,0},{32,16},{48,32},{1,49},{17,1},{33,17},{49,33},{2,50}... | collective-permute-start | bytes 589832 | tf_op jit(solution)/shard_map/ppermute | solution.py:137
  42.5 40.5 %collective-permute-start.1 = (bf16[4,12,16,128]{3,2,1,0:T(8,128)(2,1)S(1)}, bf16[4,12,16,128]{3,2,1,0:T(8,128)(2,1)S(1)}, u32[]{:S(2)}, u32[]{:S(2)}) collective-permute-start(bf16[4,12,16,128]{3,2,1,0:T(8,128)(2,1)S(1)} %slice.9), channel_id=1, source_target_pairs={{0,16},{16,32},{32,48},{48,0},{1,17},{17,33},{33,49},{49,1},{2,18}... | collective-permute-start | bytes 589832 | tf_op jit(solution)/shard_map/ppermute | solution.py:137
  73.2 20.2 %collective-permute-start.5 = (bf16[4,12,16,128]{3,2,1,0:T(8,128)(2,1)S(1)}, bf16[4,12,16,128]{3,2,1,0:T(8,128)(2,1)S(1)}, u32[]{:S(2)}, u32[]{:S(2)}) collective-permute-start(bf16[4,12,16,128]{3,2,1,0:T(8,128)(2,1)S(1)} %collective-permute-done.3), channel_id=1, source_target_pairs={{0,48},{16,0},{32,16},{48,32},{1,49},{17,1},{33,17},{49,33},{2,50}... | collective-permute-start | bytes 589832 | tf_op jit(solution)/shard_map/ppermute | solution.py:137
  77.4 18.7 %collective-permute-start.4 = (bf16[4,13,16,128]{3,2,1,0:T(8,128)(2,1)S(1)}, bf16[4,13,16,128]{3,2,1,0:T(8,128)(2,1)S(1)}, u32[]{:S(2)}, u32[]{:S(2)}) collective-permute-start(bf16[4,13,16,128]{3,2,1,0:T(8,128)(2,1)S(1)} %collective-permute-done), channel_id=1, source_target_pairs={{0,16},{16,32},{32,48},{48,0},{1,17},{17,33},{33,49},{49,1},{2,18}... | collective-permute-start | bytes 638984 | tf_op jit(solution)/shard_map/ppermute | solution.py:137
  96.2 5.7 %collective-permute-start.6 = (bf16[3,4,25,16,128]{4,3,2,1,0:T(8,128)(2,1)}, bf16[3,4,25,16,128]{4,3,2,1,0:T(8,128)(2,1)}, u32[]{:S(2)}, u32[]{:S(2)}) collective-permute-start(bf16[3,4,25,16,128]{4,3,2,1,0:T(8,128)(2,1)} %pad_maximum_fusion.refs_0_), channel_id=1, source_target_pairs={{0,64},{64,0},{1,65},{65,1},{2,66},{66,2},{3,67},{67,3},{4,68},{68... | collective-permute-start | bytes 3686408 | tf_op jit(solution)/shard_map/ppermute | solution.py:141
  98.1 3.8 %collective-permute-start.7 = (bf16[4,25,16,128]{3,2,1,0:T(8,128)(2,1)S(1)}, bf16[4,25,16,128]{3,2,1,0:T(8,128)(2,1)S(1)}, u32[]{:S(2)}, u32[]{:S(2)}) collective-permute-start(bf16[4,25,16,128]{3,2,1,0:T(8,128)(2,1)S(1)} %pad_maximum_fusion.1.refs_1_), channel_id=1, source_target_pairs={{0,64},{64,0},{1,65},{65,1},{2,66},{66,2},{3,67},{67,3},{4,68},{68... | collective-permute-start | bytes 1228808 | tf_op jit(solution)/shard_map/ppermute | solution.py:141
